TPU v7x, 256 devices: a whole 4x4x8 slice. The times are simulated.
256 devices in a mesh: seq: 32 (over x, z), tp: 4 (over y), grp: 2 (over core).
Axes of the slice: x: 4, y: 4, z: 8, core: 2. Of those that a mesh axis runs over, the one named last changes fastest.
Arguments:
- queries: bfloat16 [16384, 4096], P(('seq', 'grp'), 'tp'), may hold values from -40 to 40
- out_grad: bfloat16 [16384, 4096], P(('seq', 'grp'), 'tp'), may hold values from -6 to 6
- query_gain: float32 [128], replicated, may hold values from 0.1 to 1.9
- key_gain: float32 [128], replicated, may hold values from 0.1 to 1.9
- key_weight: bfloat16 [1024, 4096], P(None, 'tp'), may hold values from -1 to 1
- value_weight: bfloat16 [1024, 4096], P(None, 'tp'), may hold values from -0.1875 to 0.1875
- neighbours: bfloat16 [128, 2048, 1024], P(('tp', 'grp'), 'seq'), may hold values from -30 to 30
- neighbour_owner: int32 [256, 2], P(('seq', 'grp')), may hold values from 0 to 31, as said below
- owner_slots: int32 [2048], P('seq'), may hold values from -1 to 511, as said below
Outputs:
- query_grad: bfloat16 [16384, 4096], P(('seq', 'grp'), 'tp')
- neighbour_grad: bfloat16 [128, 2048, 1024], P(('tp', 'grp'), 'seq')
Inputs may be any that keep to these rules, and one draw needn't show every extreme that they name: `neighbour_owner`: entry [u, k] is the owner, an index along seq, that holds the k-th neighbour of stretch u. Among the 8 neighbours of the stretches of one index of seq and grp, no owner appears more than 1 times, and in every draw one owner appears exactly 1 times for every such index. `owner_slots`: entries o * 64 to o * 64 + 63 are the slots of owner o; each holds a neighbour number u * 2 + k or -1 where it is empty. Every neighbour is held by exactly one slot of the owner that neighbour_owner names, and one owner's slots are all full in every draw.
All inputs are finite; a program needn't handle non-finite values.
Results may differ from a plain program's by a relative error of at most 0.015.
Values may be sent and summed in bfloat16 or wider, within the bound.
A program may use at most 128 MiB of HBM per device.

v0:
```python
import math

import jax
import jax.numpy as jnp
from jax import lax
from jax.sharding import PartitionSpec as P

HD = 128
CH = 64
NB = 2


EPS = 1e-06


def scale_rows(entries, gain_vector):
    inverse = lax.rsqrt(jnp.mean(entries * entries, axis=-1, keepdims=True) + EPS)
    return entries * inverse * gain_vector


def scale_back(entries, gain_vector, upstream):
    inverse = lax.rsqrt(jnp.mean(entries * entries, axis=-1, keepdims=True) + EPS)
    scaled = upstream * gain_vector
    inner = jnp.mean(entries * scaled, axis=-1, keepdims=True)
    return inverse * scaled - entries * (inverse * inverse * inverse) * inner


def shards(
    queries,
    out_grad,
    query_gain,
    key_gain,
    key_weight,
    value_weight,
    neighbours,
    neighbour_owner,
    owner_slots,
):
    tok_rows, col_width = queries.shape
    heads_dev = col_width // HD
    stretches_dev = tok_rows // CH
    per_dev = stretches_dev * NB
    seq_count = lax.axis_size("seq")
    grp_count = lax.axis_size("grp")
    slot_count = owner_slots.shape[0]
    pair_cap = slot_count // (grp_count * seq_count)
    slot_span = seq_count * pair_cap
    rows_own = neighbours.shape[0]
    rows_tp = rows_own * grp_count
    enc_width = neighbours.shape[2]
    score_scale = 1.0 / math.sqrt(HD)
    occupied = owner_slots >= 0
    target_dev = jnp.where(occupied, owner_slots // NB // stretches_dev, -1)
    dest_seq = target_dev // grp_count
    dest_grp = target_dev % grp_count
    slot_order = jnp.arange(slot_count, dtype=jnp.int32)
    same_dest = (target_dev[:, None] == target_dev[None, :]) & (
        owner_slots[None, :] < owner_slots[:, None]
    )
    pair_rank = jnp.sum(same_dest.astype(jnp.int32), axis=1)
    target = jnp.where(occupied, dest_grp * slot_span + dest_seq * pair_cap + pair_rank, -1)
    chooser = (
        (slot_order[:, None] == target[None, :])
        .astype(jnp.bfloat16)
        .reshape(grp_count, slot_span, slot_count)
    )
    outgoing = jnp.einsum(
        "gqs,rsd->rgqd", chooser, neighbours, preferred_element_type=jnp.float32
    ).astype(jnp.bfloat16)
    arrived = lax.all_to_all(
        lax.all_to_all(outgoing, "seq", split_axis=2, concat_axis=2, tiled=True),
        "grp",
        split_axis=1,
        concat_axis=0,
        tiled=True,
    )
    arrived = arrived.reshape(rows_tp, slot_span, enc_width)
    owners = neighbour_owner.reshape(-1)
    positions = jnp.arange(per_dev, dtype=jnp.int32)
    earlier = (owners[:, None] == owners[None, :]) & (positions[None, :] < positions[:, None])
    picked = owners * pair_cap + jnp.sum(earlier.astype(jnp.int32), axis=1)
    both_weight = jnp.concatenate((key_weight, value_weight), axis=1)
    used_rows = jnp.take(arrived, picked, axis=1)
    shard_piece = lax.all_gather(used_rows, "tp", axis=0, tiled=True)
    flattened = shard_piece.reshape(-1, enc_width)
    result = jnp.dot(flattened, both_weight, preferred_element_type=jnp.float32)
    projected = result.reshape(shard_piece.shape[0], shard_piece.shape[1], 2 * col_width)
    total_rows = projected.shape[0]
    raw_keys = projected[..., :col_width].reshape(total_rows, stretches_dev, NB, heads_dev, HD)
    key_rows = scale_rows(raw_keys, key_gain).astype(jnp.bfloat16)
    value_rows = (
        projected[..., col_width:]
        .astype(jnp.bfloat16)
        .reshape(total_rows, stretches_dev, NB, heads_dev, HD)
    )
    query_raw = queries.astype(jnp.float32).reshape(stretches_dev, CH, heads_dev, HD)
    query_norm = scale_rows(query_raw, query_gain).astype(jnp.bfloat16)
    grad_out = out_grad.reshape(stretches_dev, CH, heads_dev, HD)
    scores = (
        jnp.einsum("cihd,rckhd->chikr", query_norm, key_rows, preferred_element_type=jnp.float32)
        * score_scale
    )
    weights = jnp.exp(scores)
    probability = weights / jnp.sum(weights, axis=(3, 4), keepdims=True)
    prob_grad = jnp.einsum(
        "cihd,rckhd->chikr", grad_out, value_rows, preferred_element_type=jnp.float32
    )
    inner_sum = jnp.sum(probability * prob_grad, axis=(3, 4), keepdims=True)
    score_grad = (probability * (prob_grad - inner_sum)).astype(jnp.bfloat16)
    prob_low = probability.astype(jnp.bfloat16)
    value_back = jnp.einsum(
        "chikr,cihd->rckhd", prob_low, grad_out, preferred_element_type=jnp.float32
    ).astype(jnp.bfloat16)
    key_back = (
        jnp.einsum("chikr,cihd->rckhd", score_grad, query_norm, preferred_element_type=jnp.float32)
        * score_scale
    )
    query_back = (
        jnp.einsum("chikr,rckhd->cihd", score_grad, key_rows, preferred_element_type=jnp.float32)
        * score_scale
    )
    query_grad = (
        scale_back(query_raw, query_gain, query_back)
        .astype(jnp.bfloat16)
        .reshape(tok_rows, col_width)
    )
    raw_grad = (
        scale_back(raw_keys, key_gain, key_back)
        .astype(jnp.bfloat16)
        .reshape(total_rows, per_dev, col_width)
    )
    value_grad = value_back.reshape(total_rows, per_dev, col_width)
    part_key = raw_grad.reshape(-1, col_width)
    part_value = value_grad.reshape(-1, col_width)
    contract = (((1,), (1,)), ((), ()))
    term_rows = lax.dot_general(part_key, key_weight, contract, preferred_element_type=jnp.float32)
    term_rows = term_rows + lax.dot_general(
        part_value, value_weight, contract, preferred_element_type=jnp.float32
    )
    summed = lax.psum_scatter(
        term_rows.reshape(lax.axis_size("tp") * rows_tp, per_dev, enc_width).astype(jnp.bfloat16),
        "tp",
        scatter_dimension=0,
        tiled=True,
    )
    outbound = jnp.zeros((rows_tp, slot_span, enc_width), jnp.bfloat16).at[:, picked].set(summed)
    outbound = outbound.reshape(rows_tp, 1, slot_span, enc_width)
    returned = lax.all_to_all(
        lax.all_to_all(outbound, "seq", split_axis=2, concat_axis=2, tiled=True),
        "grp",
        split_axis=0,
        concat_axis=1,
        tiled=True,
    )
    neighbour_grad = jnp.einsum(
        "gqs,rgqd->rsd", chooser, returned, preferred_element_type=jnp.float32
    ).astype(jnp.bfloat16)
    return (query_grad, neighbour_grad)


def solution(mesh):
    in_specs = (
        P(("seq", "grp"), "tp"),
        P(("seq", "grp"), "tp"),
        P(),
        P(),
        P(None, "tp"),
        P(None, "tp"),
        P(("tp", "grp"), "seq", None),
        P(("seq", "grp"), None),
        P("seq"),
    )
    out_specs = (P(("seq", "grp"), "tp"), P(("tp", "grp"), "seq", None))
    return jax.shard_map(shards, mesh=mesh, in_specs=in_specs, out_specs=out_specs, check_vma=False)
```

profile of v0, /device:TPU:1, one launch (start us, length us, event | category | flops | bytes accessed | tf_op | source)
XLA Modules:
  0.0 284.8 jit_solution(4379356542337011692)
XLA Ops:
  7.2 0.8 compare_select_fusion.12
  8.0 0.9 convert_reduce_fusion
  8.9 0.7 compare_select_fusion.11
  9.6 0.8 convert_bitcast_fusion.1
  10.4 2.5 copy.128
  12.9 12.0 %all-to-all-start = ((bf16[16,2,32,1024]{3,0,1,2:T(8,128)(2,1)}), bf16[16,2,32,1024]{3,0,1,2:T(8,128)(2,1)S(1)}, u32[]{:S(2)}, u32[]{:S(2)}) async-start(bf16[16,2,32,1024]{3,0,1,2:T(8,128)(2,1)} %copy.128), calls=%async_computation | async-start | bytes 4194304 | tf_op jit(solution)/shard_map/all_to_all | solution.py:71
  25.2 0.2 convert_reduce_fusion.1
  25.4 48.4 %all-to-all-done = bf16[16,2,32,1024]{3,0,1,2:T(8,128)(2,1)S(1)} async-done(((bf16[16,2,32,1024]{3,0,1,2:T(8,128)(2,1)}), bf16[16,2,32,1024]{3,0,1,2:T(8,128)(2,1)S(1)}, u32[]{:S(2)}, u32[]{:S(2)}) %all-to-all-start) | async-done | bytes 2097184 | tf_op jit(solution)/shard_map/all_to_all | solution.py:71
  73.9 7.1 %all_to_all.43 = bf16[16,2,32,1024]{3,0,2,1:T(8,128)(2,1)S(1)} all-to-all(bf16[16,2,32,1024]{3,0,2,1:T(8,128)(2,1)S(1)} %copy.129), channel_id=1, replica_groups=mesh['seq'=32,'tp'=4,'grp'=2] {'grp'}, dimensions={1} | all-to-all | bytes 4194304 | tf_op jit(solution)/shard_map/all_to_all | solution.py:70
  81.1 1.6 copy.130
  82.7 2.2 gather_fusion
  84.9 0.9 select_bitcast_fusion
  86.1 0.2 copy.165
  86.3 0.3 multiply_reduce_fusion.2
  86.7 0.4 copy-done.6
  87.3 29.7 %all-gather.2.cloned.1.call-done = bf16[128,8,1024]{2,0,1:T(8,128)(2,1)} async-done(((bf16[32,8,1024]{2,0,1:T(8,128)(2,1)}), bf16[128,8,1024]{2,0,1:T(8,128)(2,1)}) %all-gather.2.cloned.1.call-update) | async-done | bytes 2097168 | tf_op jit(solution)/shard_map/all_gather | solution.py:84
  116.9 7.1 %fusion = f32[128,8,2048]{2,0,1:T(8,128)S(1)} fusion(bf16[128,8,1024]{2,0,1:T(8,128)(2,1)} %all-gather.2.cloned.1.call-done, bf16[1024,1024]{1,0:T(8,128)(2,1)} %param.14, bf16[1024,1024]{1,0:T(8,128)(2,1)} %param.13), kind=kOutput, calls=%fused_computation.4 | convolution fusion | flops 4303355904 | bytes 14680064 | tf_op jit(solution)/shard_map/dot_general | solution.py:86
  124.0 0.3 slice.11
  124.3 2.9 %copy-done.3 = f32[128,8,2048]{2,0,1:T(8,128)} copy-done((f32[128,8,2048]{2,0,1:T(8,128)}, f32[128,8,2048]{2,0,1:T(8,128)S(1)}, u32[]{:S(2)}) %copy-start.3) | copy-done | bytes 8388632
  127.2 3.0 %copy.166 = f32[128,8,8,128]{3,2,1,0:T(8,128)} copy(f32[128,8,8,128]{3,1,2,0:T(8,128)S(1)} %bitcast.151) | data formatting | bytes 8388608
  130.2 5.3 %copy.134 = f32[128,4,2,8,128]{0,4,2,3,1:T(8,128)} copy(f32[128,4,2,8,128]{4,3,0,2,1:T(8,128)} %bitcast.144) | data formatting | bytes 8388608 | tf_op jit(solution)/shard_map/reshape | solution.py:89
  135.5 3.4 %multiply_reduce_fusion = f32[128,4,2,8]{3,0,2,1:T(8,128)S(1)} fusion(f32[128,4,2,8,128]{4,3,0,2,1:T(8,128)} %bitcast.145), kind=kLoop, calls=%fused_computation.15 | loop fusion | flops 2088960 | bytes 4227072 | tf_op jit(solution)/shard_map/reduce_sum | solution.py:17
  138.8 3.8 %slice.14 = bf16[128,8,1024]{2,0,1:T(8,128)(2,1)} slice(f32[128,8,2048]{2,0,1:T(8,128)} %copy-done.3), slice={[0:128], [0:8], [1024:2048]} | slice | bytes 4194304 | tf_op jit(solution)/shard_map/slice | solution.py:92
  142.9 2.4 copy.167
  145.3 0.4 copy-done.2
  145.7 1.2 bitcast_reduce_fusion
  146.9 2.5 convert_bitcast_fusion
  149.4 1.2 fusion.13
  150.7 0.7 fusion.15
  151.4 1.4 fusion.5
  152.8 3.0 %fusion.4 = bf16[128,4,2,8,128]{0,4,2,3,1:T(8,128)(2,1)} fusion(f32[128,4,2,8,128]{0,4,2,3,1:T(8,128)S(1)} %copy-done.2, f32[4,8,128,2,128]{4,2,3,1,0:T(8,128)S(1)} %get-tuple-element.13, f32[128,4,2,8]{0,2,3,1:T(2,128)S(1)} %copy.147, f32[128,4,2,8]{0,2,3,1:T(2,128)S(1)} %copy.143, f32[128]{0:T(128)S(1)} %broadcast_multiply_fusion.1, ...), kind=kLoop, calls=%fused_computation.11 | loop fusion | flops 6291456 | bytes 10584576 | tf_op jit(solution)/shard_map/convert_element_type | solution.py:129
  155.8 4.6 %copy.148 = bf16[128,4,2,8,128]{4,3,2,1,0:T(8,128)(2,1)} copy(bf16[128,4,2,8,128]{0,4,2,3,1:T(8,128)(2,1)} %fusion.4) | data formatting | bytes 4194304 | tf_op jit(solution)/shard_map/convert_element_type | solution.py:129
  160.3 3.1 %copy.150 = bf16[128,4,2,8,128]{4,3,2,1,0:T(8,128)(2,1)S(1)} copy(bf16[128,4,2,8,128]{4,0,2,3,1:T(8,128)(2,1)} %convert_bitcast_fusion) | data formatting | bytes 4194304 | tf_op jit(solution)/shard_map/convert_element_type | solution.py:113
  163.5 2.4 fusion.7
  165.9 2.4 fusion.6
  168.2 2.5 copy.151
  170.7 32.5 %reduce-scatter.2.cloned.1.call-done = bf16[32,8,1024]{2,0,1:T(8,128)(2,1)} async-done(((bf16[128,8,1024]{2,0,1:T(8,128)(2,1)}), bf16[32,8,1024]{2,0,1:T(8,128)(2,1)}) %reduce-scatter.2.cloned.1.call-update) | async-done | bytes 524304 | tf_op jit(solution)/shard_map/reduce_scatter | solution.py:140
  203.2 1.6 broadcast_in_dim.17
  204.8 2.4 scatter_fusion
  207.3 9.6 %all-to-all-start.2 = ((bf16[32,1,32,1024]{3,0,1,2:T(8,128)(2,1)}), bf16[32,1,32,1024]{3,0,1,2:T(8,128)(2,1)}, u32[]{:S(2)}, u32[]{:S(2)}) async-start(bf16[32,1,32,1024]{3,0,1,2:T(8,128)(2,1)} %bitcast.152), calls=%async_computation.3 | async-start | bytes 4194304 | tf_op jit(solution)/shard_map/all_to_all | solution.py:149
  216.9 3.2 %multiply_reduce_fusion.1 = (f32[4,64,8]{1,2,0:T(8,128)S(1)}, f32[4,64,8,128]{3,1,2,0:T(8,128)S(1)}) fusion(f32[4,64,8,128]{3,2,1,0:T(8,128)S(1)} %bitcast.149, f32[128]{0:T(128)S(1)} %broadcast_multiply_fusion.2, bf16[4,8,64,2,128]{4,2,3,1,0:T(8,128)(2,1)S(1)} %fusion.15, f32[128,4,2,8,128]{0,4,2,3,1:T(8,128)} %copy.134, f32[128]{0:T(128)S(1)} %copy-done.9, ...), kind=kOutput, calls=%fused_computation.44 | convolution fusion | flops 138147840 | bytes 7382016 | tf_op jit(solution)/shard_map/chikr,rckhd->cihd/dot_general | solution.py:119
  220.1 1.0 subtract_convert_fusion
  221.1 0.3 copy.142
  221.5 0.9 copy.205
  222.4 43.4 %all-to-all-done.2 = bf16[32,1,32,1024]{3,0,1,2:T(8,128)(2,1)} async-done(((bf16[32,1,32,1024]{3,0,1,2:T(8,128)(2,1)}), bf16[32,1,32,1024]{3,0,1,2:T(8,128)(2,1)}, u32[]{:S(2)}, u32[]{:S(2)}) %all-to-all-start.2) | async-done | bytes 2097184 | tf_op jit(solution)/shard_map/all_to_all | solution.py:149
  265.7 2.7 copy.153
  268.5 7.2 %all_to_all.44 = bf16[32,1,32,1024]{3,2,1,0:T(8,128)(2,1)S(1)} all-to-all(bf16[32,1,32,1024]{3,2,1,0:T(8,128)(2,1)S(1)} %copy.153), channel_id=1, replica_groups=mesh['seq'=32,'tp'=4,'grp'=2] {'grp'}, dimensions={0} | all-to-all | bytes 4194304 | tf_op jit(solution)/shard_map/all_to_all | solution.py:148
  275.7 2.2 fusion.24
  (49 shorter events, 1.2 us)
Async XLA Ops:
  7.2 2.5 copy-start
  12.9 12.0 %copy-start.10 = (s32[4,2]{0,1:T(2,128)S(1)}, s32[4,2]{0,1:T(2,128)}, u32[]{:S(2)}) copy-start(s32[4,2]{0,1:T(2,128)} %param.16) | copy-start | bytes 100
  12.9 60.9 %all-to-all-start = ((bf16[16,2,32,1024]{3,0,1,2:T(8,128)(2,1)}), bf16[16,2,32,1024]{3,0,1,2:T(8,128)(2,1)S(1)}, u32[]{:S(2)}, u32[]{:S(2)}) async-start(bf16[16,2,32,1024]{3,0,1,2:T(8,128)(2,1)} %copy.128), calls=%async_computation | async-start | bytes 4194304 | tf_op jit(solution)/shard_map/all_to_all | solution.py:71
  24.9 92.1 %all-gather.2.cloned.1.call-start = ((), (), s32[]{:S(2)}) async-start(), calls=%async_computation.5 | async-start | bytes 2621440 | tf_op jit(solution)/shard_map/all_gather | solution.py:84
  82.7 3.2 %copy-start.5 = (bf16[256,1024]{1,0:T(8,128)(2,1)S(1)}, bf16[256,1024]{1,0:T(8,128)(2,1)}, u32[]{:S(2)}) copy-start(bf16[256,1024]{1,0:T(8,128)(2,1)} %param.9) | copy-start | bytes 1572868
  85.9 117.4 %reduce-scatter.2.cloned.1.call-start = ((), (), s32[]{:S(2)}) async-start(), calls=%async_computation.6 | async-start | bytes 2621440 | tf_op jit(solution)/shard_map/reduce_scatter | solution.py:140
  86.1 1.0 copy-start.6
  86.1 1.1 copy-start.9
  124.0 3.2 %copy-start.3 = (f32[128,8,2048]{2,0,1:T(8,128)}, f32[128,8,2048]{2,0,1:T(8,128)S(1)}, u32[]{:S(2)}) copy-start(f32[128,8,2048]{2,0,1:T(8,128)S(1)} %fusion) | copy-start | bytes 25165828
  142.9 2.8 copy-start.2
  142.9 2.8 copy-start.8
  160.3 3.1 %copy-start.11 = (bf16[1024,1024]{1,0:T(8,128)(2,1)S(1)}, bf16[1024,1024]{1,0:T(8,128)(2,1)}, u32[]{:S(2)}) copy-start(bf16[1024,1024]{1,0:T(8,128)(2,1)} %param.14) | copy-start | bytes 6291460
  163.4 2.4 copy-start.4
  163.5 2.4 copy-start.12
  203.2 1.6 copy-start.7
  207.3 58.5 %all-to-all-start.2 = ((bf16[32,1,32,1024]{3,0,1,2:T(8,128)(2,1)}), bf16[32,1,32,1024]{3,0,1,2:T(8,128)(2,1)}, u32[]{:S(2)}, u32[]{:S(2)}) async-start(bf16[32,1,32,1024]{3,0,1,2:T(8,128)(2,1)} %bitcast.152), calls=%async_computation.3 | async-start | bytes 4194304 | tf_op jit(solution)/shard_map/all_to_all | solution.py:149
  275.7 2.2 copy-start.1
Sparse Core Ops, SparseCore 0:
  86.0 30.8 all-gather.1
  170.9 32.3 reduce-scatter.1
where the time goes:
time: 286 us; the launch traced here: 285 us
  waiting for transfers between devices  154 us (54%)
  local copies, waits for them, and re-layouts  44 us (15%)
  matrix products  24.3 us (8%)
  starting transfers between devices  21.7 us (8%)
  between operations  14.4 us (5%)
  blocking collectives  14.3 us (5%)
  other arithmetic  12.1 us (4%)
    all_to_all x1, waiting for transfers between devices, shards(): lax.all_to_all(outgoing, 'seq', split_axis=2, concat_axis=2, tiled=True)  48.4 us
    all_to_all x1, waiting for transfers between devices, shards(): lax.all_to_all(outbound, 'seq', split_axis=2, concat_axis=2, tiled=True)  43.4 us
    reduce_scatter x1, waiting for transfers between devices, shards(): lax.psum_scatter(term_rows.reshape(lax.axis_size('tp') * rows_tp, per_dev...  32.5 us
    all_gather x1, waiting for transfers between devices, shards(): shard_piece = lax.all_gather(used_rows, 'tp', axis=0, tiled=True)  29.7 us
    all_to_all x1, starting transfers between devices, shards(): lax.all_to_all(outgoing, 'seq', split_axis=2, concat_axis=2, tiled=True)  12 us
    unnamed x32, local copies, waits for them, and re-layouts  10.4 us
    all_to_all x1, starting transfers between devices, shards(): lax.all_to_all(outbound, 'seq', split_axis=2, concat_axis=2, tiled=True)  9.65 us
    all_to_all x1, blocking collectives, shards(): lax.all_to_all(lax.all_to_all(outbound, 'seq', split_axis=2, concat_axis=...  7.22 us
  transfers between devices with their start and end apart: 4, of which 4 were waited for; matrix products, arithmetic and copies ran while one was open for 2% of the time, Pallas kernels for 0%

commit v1 on v0

v1 whole, which is shorter than its diff:
```python
import math

import jax
import jax.numpy as jnp
from jax import lax
from jax.experimental import pallas as pl
from jax.experimental.pallas import tpu as pltpu
from jax.sharding import PartitionSpec as P

HD = 128
CH = 64
NB = 2


EPS = 1e-06
SCALE = 1.0 / math.sqrt(HD)
NT = (((1,), (1,)), ((), ()))
TN = (((0,), (0,)), ((), ()))
NN = (((1,), (0,)), ((), ()))


def dot(a, b, dims):
    return lax.dot_general(a, b, dims, preferred_element_type=jnp.float32)


def attend(e_ref, wk_ref, wv_ref, q_ref, go_ref, qg_ref, kg_ref, qgrad_ref, dkr_ref, dv_ref):
    rows, width = q_ref.shape
    stretches = rows // CH
    groups, per_dev, sub, enc = e_ref.shape
    keys = groups * 2 * sub
    qgain = qg_ref[...]
    kgain = kg_ref[...]

    def pair(i, carry):
        cols = pl.ds(pl.multiple_of(i * 2 * HD, 2 * HD), 2 * HD)
        enc_rows = e_ref[...].reshape(groups * per_dev * sub, enc)
        kr2 = dot(enc_rows, wk_ref[:, cols], NN)
        val2 = dot(enc_rows, wv_ref[:, cols], NN).astype(jnp.bfloat16)
        for hh in range(2):
            lanes = slice(hh * HD, (hh + 1) * HD)
            head = pl.ds(pl.multiple_of((i * 2 + hh) * HD, HD), HD)
            kr = kr2[:, lanes]
            val = val2[:, lanes].reshape(groups, per_dev, sub, HD)
            kinv = lax.rsqrt(jnp.mean(kr * kr, axis=-1, keepdims=True) + EPS)
            khat = kr * kinv
            kn = (khat * kgain).astype(jnp.bfloat16).reshape(groups, per_dev, sub, HD)
            khat = khat.reshape(groups, per_dev, sub, HD)
            kinv = kinv.reshape(groups, per_dev, sub, 1)
            qx = q_ref[:, head].astype(jnp.float32)
            qinv = lax.rsqrt(jnp.mean(qx * qx, axis=-1, keepdims=True) + EPS)
            qhat = qx * qinv
            qn = (qhat * qgain).astype(jnp.bfloat16)
            go = go_ref[:, head]
            for c in range(stretches):
                tok = slice(c * CH, (c + 1) * CH)
                kn_c = kn[:, 2 * c:2 * c + 2].reshape(keys, HD)
                val_c = val[:, 2 * c:2 * c + 2].reshape(keys, HD)
                qn_c, go_c = qn[tok], go[tok]
                weights = jnp.exp(dot(qn_c, kn_c, NT) * SCALE)
                prob = weights * (1.0 / jnp.sum(weights, axis=-1, keepdims=True))
                dp = dot(go_c, val_c, NT)
                inner = jnp.sum(prob * dp, axis=-1, keepdims=True)
                ds = (prob * (dp - inner)).astype(jnp.bfloat16)
                pb = prob.astype(jnp.bfloat16)
                dv_c = dot(pb, go_c, TN).astype(jnp.bfloat16)
                dkn = dot(ds, qn_c, TN)
                dqn = dot(ds, kn_c, NN)
                qs = dqn * (qgain * SCALE)
                qh = qhat[tok]
                qi = jnp.mean(qh * qs, axis=-1, keepdims=True)
                qgrad_ref[tok, head] = (qinv[tok] * (qs - qh * qi)).astype(jnp.bfloat16)
                ks = dkn * (kgain * SCALE)
                kh = khat[:, 2 * c:2 * c + 2].reshape(keys, HD)
                ki = jnp.mean(kh * ks, axis=-1, keepdims=True)
                kv = kinv[:, 2 * c:2 * c + 2].reshape(keys, 1)
                dk = (kv * (ks - kh * ki)).astype(jnp.bfloat16)
                dkr_ref[:, 2 * c:2 * c + 2, :, head] = dk.reshape(groups, 2, sub, HD)
                dv_ref[:, 2 * c:2 * c + 2, :, head] = dv_c.reshape(groups, 2, sub, HD)
        return carry
    lax.fori_loop(0, width // (2 * HD), pair, 0)


def compute_kernel(e_ref, wk_ref, wv_ref, q_ref, go_ref, qg_ref, kg_ref, qgrad_ref, de_ref, dkr_ref, dv_ref):
    attend(e_ref, wk_ref, wv_ref, q_ref, go_ref, qg_ref, kg_ref, qgrad_ref, dkr_ref, dv_ref)
    groups, per_dev, sub, enc = e_ref.shape
    width = q_ref.shape[1]

    def back(j, carry):
        cols = pl.ds(pl.multiple_of(j * 256, 256), 256)
        total = dot(dkr_ref[...].reshape(-1, width), wk_ref[cols, :], NT)
        total = total + dot(dv_ref[...].reshape(-1, width), wv_ref[cols, :], NT)
        de_ref[:, :, :, cols] = total.astype(jnp.bfloat16).reshape(groups, per_dev, sub, 256)
        return carry
    lax.fori_loop(0, enc // 256, back, 0)


def compute(e, wk, wv, q, go, qg, kg):
    vm = pl.BlockSpec(memory_space=pltpu.VMEM)
    return pl.pallas_call(
        compute_kernel,
        out_shape=(jax.ShapeDtypeStruct(q.shape, jnp.bfloat16), jax.ShapeDtypeStruct(e.shape, jnp.bfloat16)),
        in_specs=[vm] * 7,
        out_specs=(vm, vm),
        scratch_shapes=[pltpu.VMEM(e.shape, jnp.bfloat16), pltpu.VMEM(e.shape, jnp.bfloat16)],
        name="attention",
        compiler_params=pltpu.CompilerParams(vmem_limit_bytes=56 * 2**20),
    )(e, wk, wv, q, go, qg.reshape(1, HD), kg.reshape(1, HD))


def shards(
    queries,
    out_grad,
    query_gain,
    key_gain,
    key_weight,
    value_weight,
    neighbours,
    neighbour_owner,
    owner_slots,
):
    tok_rows, col_width = queries.shape
    stretches_dev = tok_rows // CH
    per_dev = stretches_dev * NB
    seq_count = lax.axis_size("seq")
    grp_count = lax.axis_size("grp")
    slot_count = owner_slots.shape[0]
    pair_cap = slot_count // (grp_count * seq_count)
    slot_span = seq_count * pair_cap
    rows_own = neighbours.shape[0]
    rows_tp = rows_own * grp_count
    enc_width = neighbours.shape[2]
    occupied = owner_slots >= 0
    target_dev = jnp.where(occupied, owner_slots // NB // stretches_dev, -1)
    dest_seq = target_dev // grp_count
    dest_grp = target_dev % grp_count
    slot_order = jnp.arange(slot_count, dtype=jnp.int32)
    same_dest = (target_dev[:, None] == target_dev[None, :]) & (
        owner_slots[None, :] < owner_slots[:, None]
    )
    pair_rank = jnp.sum(same_dest.astype(jnp.int32), axis=1)
    target = jnp.where(occupied, dest_grp * slot_span + dest_seq * pair_cap + pair_rank, -1)
    chooser = (
        (slot_order[:, None] == target[None, :])
        .astype(jnp.bfloat16)
        .reshape(grp_count, slot_span, slot_count)
    )
    outgoing = jnp.einsum(
        "gqs,rsd->rgqd", chooser, neighbours, preferred_element_type=jnp.float32
    ).astype(jnp.bfloat16)
    arrived = lax.all_to_all(
        lax.all_to_all(outgoing, "seq", split_axis=2, concat_axis=2, tiled=True),
        "grp",
        split_axis=1,
        concat_axis=0,
        tiled=True,
    )
    arrived = arrived.reshape(rows_tp, slot_span, enc_width)
    owners = neighbour_owner.reshape(-1)
    positions = jnp.arange(per_dev, dtype=jnp.int32)
    earlier = (owners[:, None] == owners[None, :]) & (positions[None, :] < positions[:, None])
    picked = owners * pair_cap + jnp.sum(earlier.astype(jnp.int32), axis=1)
    used_rows = jnp.take(arrived, picked, axis=1)
    shard_piece = lax.all_gather(used_rows, "tp", axis=0, tiled=True)
    groups = shard_piece.shape[0] // 16
    enc = shard_piece.reshape(groups, 16, per_dev, enc_width).transpose(0, 2, 1, 3)
    query_grad, enc_grad = compute(
        enc, key_weight, value_weight, queries, out_grad, query_gain, key_gain
    )
    term_rows = enc_grad.transpose(0, 2, 1, 3)
    summed = lax.psum_scatter(
        term_rows.reshape(lax.axis_size("tp") * rows_tp, per_dev, enc_width),
        "tp",
        scatter_dimension=0,
        tiled=True,
    )
    outbound = jnp.zeros((rows_tp, slot_span, enc_width), jnp.bfloat16).at[:, picked].set(summed)
    outbound = outbound.reshape(rows_tp, 1, slot_span, enc_width)
    returned = lax.all_to_all(
        lax.all_to_all(outbound, "seq", split_axis=2, concat_axis=2, tiled=True),
        "grp",
        split_axis=0,
        concat_axis=1,
        tiled=True,
    )
    neighbour_grad = jnp.einsum(
        "gqs,rgqd->rsd", chooser, returned, preferred_element_type=jnp.float32
    ).astype(jnp.bfloat16)
    return (query_grad, neighbour_grad)


def solution(mesh):
    in_specs = (
        P(("seq", "grp"), "tp"),
        P(("seq", "grp"), "tp"),
        P(),
        P(),
        P(None, "tp"),
        P(None, "tp"),
        P(("tp", "grp"), "seq", None),
        P(("seq", "grp"), None),
        P("seq"),
    )
    out_specs = (P(("seq", "grp"), "tp"), P(("tp", "grp"), "seq", None))
    return jax.shard_map(shards, mesh=mesh, in_specs=in_specs, out_specs=out_specs, check_vma=False)
```

time: 286 us -> 270 us (0.944)
  blocking collectives: 14.3 us -> 73.8 us
  waiting for transfers between devices: 154 us -> 112 us
  Pallas kernels: 0 us -> 28.5 us
  local copies, waits for them, and re-layouts: 44 us -> 22.1 us
  matrix products: 24.3 us -> 2.97 us
  starting transfers between devices: 21.7 us -> 12.2 us
  other arithmetic: 12.1 us -> 3.55 us
    all_to_all x0 -> x1, blocking collectives: none -> 56.6 us  [shards(): lax.all_to_all(outbound, 'seq', split_axis=2, concat_axis=2, tiled=True)]
    all_to_all x1 -> x0, waiting for transfers between devices: 43.4 us -> none  [shards(): lax.all_to_all(outbound, 'seq', split_axis=2, concat_axis=2, tiled=True)]
    pallas_call x0 -> x1, Pallas kernels: none -> 28.5 us  [compute(): pl.pallas_call(compute_kernel, out_shape=(jax.ShapeDtypeStruct(q.shape, j...]
    dot_general x8 -> x0, matrix products: 21.3 us -> none  [the longest x1 7.08 us: shards(): result = jnp.dot(flattened, both_weight, preferred_element_type=jnp.float32)]
    convert_element_type x4 -> x0, local copies, waits for them, and re-layouts: 10.5 us -> none  [the longest x1 4.56 us: shards(): raw_grad = scale_back(raw_keys, key_gain, key_back).astype(jnp.bfloat16)....]
    unnamed x32 -> x5, local copies, waits for them, and re-layouts: 10.4 us -> 0.11 us
    all_to_all x1 -> x0, starting transfers between devices: 9.65 us -> none  [shards(): lax.all_to_all(outbound, 'seq', split_axis=2, concat_axis=2, tiled=True)]
    convert_element_type x3 -> x0, other arithmetic: 4.68 us -> none  [the longest x1 2.96 us: shards(): raw_grad = scale_back(raw_keys, key_gain, key_back).astype(jnp.bfloat16)....]
  transfers between devices with their start and end apart: 4 -> 3, of which waited for: 4 -> 3; matrix products, arithmetic and copies ran while one was open for 2% -> 0% of each run, Pallas kernels for 0% -> 0%
where the time goes in v1:
time: 270 us; the launch traced here: 269 us
  waiting for transfers between devices  112 us (41%)
  blocking collectives  73.8 us (27%)
  Pallas kernels  28.5 us (11%)
  local copies, waits for them, and re-layouts  22.1 us (8%)
  between operations  14.1 us (5%)
  starting transfers between devices  12.2 us (5%)
  other arithmetic  3.55 us (1%)
  matrix products  2.97 us (1%)
    all_to_all x1, blocking collectives, shards(): lax.all_to_all(outbound, 'seq', split_axis=2, concat_axis=2, tiled=True)  56.6 us
    all_to_all x1, waiting for transfers between devices, shards(): lax.all_to_all(outgoing, 'seq', split_axis=2, concat_axis=2, tiled=True)  48.3 us
    reduce_scatter x1, waiting for transfers between devices, shards(): lax.psum_scatter(term_rows.reshape(lax.axis_size('tp') * rows_tp, per_dev...  32.5 us
    all_gather x1, waiting for transfers between devices, shards(): shard_piece = lax.all_gather(used_rows, 'tp', axis=0, tiled=True)  31 us
    pallas_call x1, Pallas kernels, compute(): pl.pallas_call(compute_kernel, out_shape=(jax.ShapeDtypeStruct(q.shape, j...  28.5 us
    all_to_all x1, starting transfers between devices, shards(): lax.all_to_all(outgoing, 'seq', split_axis=2, concat_axis=2, tiled=True)  12.1 us
    all_to_all x1, blocking collectives, shards(): lax.all_to_all(lax.all_to_all(outbound, 'seq', split_axis=2, concat_axis=...  10.1 us
    all_to_all x1, blocking collectives, shards(): lax.all_to_all(lax.all_to_all(outgoing, 'seq', split_axis=2, concat_axis=...  7.14 us
  transfers between devices with their start and end apart: 3, of which 3 were waited for; matrix products, arithmetic and copies ran while one was open for 0% of the time, Pallas kernels for 0%

profile of v1, /device:TPU:1, one launch (start us, length us, event | category | flops | bytes accessed | tf_op | source)
XLA Modules:
  0.0 269.1 jit_solution(6089406696293763598)
XLA Ops:
  7.2 0.0 copy-start
  7.2 0.8 compare_select_fusion.12
  8.0 0.9 convert_reduce_fusion
  8.9 0.7 compare_select_fusion.11
  9.6 0.0 copy-done
  9.6 0.7 convert_bitcast_fusion
  10.4 2.5 copy.43
  12.8 0.0 copy-start.1
  12.9 12.1 %all-to-all-start = ((bf16[16,2,32,1024]{3,0,1,2:T(8,128)(2,1)}), bf16[16,2,32,1024]{3,0,1,2:T(8,128)(2,1)}, u32[]{:S(2)}, u32[]{:S(2)}) async-start(bf16[16,2,32,1024]{3,0,1,2:T(8,128)(2,1)} %copy.43), calls=%async_computation | async-start | bytes 4194304 | tf_op jit(solution)/shard_map/all_to_all | solution.py:151
  25.0 0.0 all-gather.2.cloned.1.call-start
  25.0 0.0 copy-done.1
  25.1 0.1 copy.42
  25.1 0.1 reshape.83
  25.2 0.1 reshape.85
  25.3 0.2 convert_reduce_fusion.1
  25.5 48.3 %all-to-all-done = bf16[16,2,32,1024]{3,0,1,2:T(8,128)(2,1)} async-done(((bf16[16,2,32,1024]{3,0,1,2:T(8,128)(2,1)}), bf16[16,2,32,1024]{3,0,1,2:T(8,128)(2,1)}, u32[]{:S(2)}, u32[]{:S(2)}) %all-to-all-start) | async-done | bytes 2097184 | tf_op jit(solution)/shard_map/all_to_all | solution.py:151
  73.9 1.8 copy.44
  75.6 7.1 %all_to_all.43 = bf16[16,2,32,1024]{3,0,2,1:T(8,128)(2,1)S(1)} all-to-all(bf16[16,2,32,1024]{3,0,2,1:T(8,128)(2,1)S(1)} %copy.44), channel_id=1, replica_groups=mesh['seq'=32,'tp'=4,'grp'=2] {'grp'}, dimensions={1} | all-to-all | bytes 4194304 | tf_op jit(solution)/shard_map/all_to_all | solution.py:150
  82.8 1.5 copy.45
  84.3 2.2 gather_fusion
  86.4 0.9 select_bitcast_fusion
  87.4 0.0 all-gather.2.cloned.1.call-update
  87.4 0.0 reduce-scatter.2.cloned.1.call-start
  87.4 31.0 %all-gather.2.cloned.1.call-done = bf16[128,8,1024]{2,0,1:T(8,128)(2,1)} async-done(((bf16[32,8,1024]{2,0,1:T(8,128)(2,1)}), bf16[128,8,1024]{2,0,1:T(8,128)(2,1)}) %all-gather.2.cloned.1.call-update) | async-done | bytes 2097168 | tf_op jit(solution)/shard_map/all_gather | solution.py:163
  118.4 3.2 %copy.57 = bf16[8,16,8,1024]{3,1,2,0:T(8,128)(2,1)} copy(bf16[8,16,8,1024]{3,1,0,2:T(8,128)(2,1)} %bitcast.57) | data formatting | bytes 4194304 | tf_op jit(solution)/shard_map/reshape | solution.py:165
  121.7 28.5 %attention.1 = (bf16[256,1024]{1,0:T(8,128)(2,1)}, bf16[8,8,16,1024]{3,2,1,0:T(8,128)(2,1)}) custom-call(bf16[8,8,16,1024]{3,2,1,0:T(8,128)(2,1)} %bitcast.55, bf16[1024,1024]{1,0:T(8,128)(2,1)} %wk_ref.1, bf16[1024,1024]{1,0:T(8,128)(2,1)} %wv_ref.1, bf16[256,1024]{1,0:T(8,128)(2,1)} %q_ref.1, bf16[256,1024]{1,0:T(8,128)(2,1)} %go_ref.1, ...), custom_call_target="tpu_custom_call" | custom-call | tf_op jit(solution)/shard_map/attention/pallas_call | solution.py:99
  150.2 4.2 %copy.49 = bf16[8,16,8,1024]{3,2,1,0:T(8,128)(2,1)} copy(bf16[8,16,8,1024]{3,1,2,0:T(8,128)(2,1)} %bitcast.58) | data formatting | bytes 4194304 | tf_op jit(solution)/shard_map/transpose | solution.py:169
  154.3 0.0 reduce-scatter.2.cloned.1.call-update
  154.4 32.5 %reduce-scatter.2.cloned.1.call-done = bf16[32,8,1024]{2,1,0:T(8,128)(2,1)} async-done(((bf16[128,8,1024]{2,1,0:T(8,128)(2,1)}), bf16[32,8,1024]{2,1,0:T(8,128)(2,1)}) %reduce-scatter.2.cloned.1.call-update) | async-done | bytes 524304 | tf_op jit(solution)/shard_map/reduce_scatter | solution.py:170
  186.9 1.3 copy.50
  188.2 1.6 broadcast_in_dim.17
  189.8 2.5 scatter_fusion
  192.2 56.6 %all_to_all.44 = bf16[32,1,32,1024]{3,0,1,2:T(8,128)(2,1)S(1)} all-to-all(bf16[32,1,32,1024]{3,0,1,2:T(8,128)(2,1)} %bitcast.51), channel_id=1, replica_groups=mesh['seq'=32,'tp'=4,'grp'=2] {'seq'}, dimensions={2} | all-to-all | bytes 4194304 | tf_op jit(solution)/shard_map/all_to_all | solution.py:179
  248.8 1.2 copy.52
  250.0 10.1 %all_to_all.45 = bf16[32,1,32,1024]{3,2,1,0:T(8,128)(2,1)S(1)} all-to-all(bf16[32,1,32,1024]{3,2,1,0:T(8,128)(2,1)S(1)} %copy.52), channel_id=1, replica_groups=mesh['seq'=32,'tp'=4,'grp'=2] {'grp'}, dimensions={0} | all-to-all | bytes 4194304 | tf_op jit(solution)/shard_map/all_to_all | solution.py:178
  260.1 2.2 fusion.4
  (4 shorter events, 0.0 us)
Async XLA Ops:
  7.2 2.5 copy-start
  12.8 12.2 %copy-start.1 = (s32[4,2]{0,1:T(2,128)S(1)}, s32[4,2]{0,1:T(2,128)}, u32[]{:S(2)}) copy-start(s32[4,2]{0,1:T(2,128)} %param.16) | copy-start | bytes 100
  12.9 61.0 %all-to-all-start = ((bf16[16,2,32,1024]{3,0,1,2:T(8,128)(2,1)}), bf16[16,2,32,1024]{3,0,1,2:T(8,128)(2,1)}, u32[]{:S(2)}, u32[]{:S(2)}) async-start(bf16[16,2,32,1024]{3,0,1,2:T(8,128)(2,1)} %copy.43), calls=%async_computation | async-start | bytes 4194304 | tf_op jit(solution)/shard_map/all_to_all | solution.py:151
  25.0 93.4 %all-gather.2.cloned.1.call-start = ((), (), s32[]{:S(2)}) async-start(), calls=%async_computation.5 | async-start | bytes 2621440 | tf_op jit(solution)/shard_map/all_gather | solution.py:163
  87.4 99.5 %reduce-scatter.2.cloned.1.call-start = ((), (), s32[]{:S(2)}) async-start(), calls=%async_computation.6 | async-start | bytes 2621440 | tf_op jit(solution)/shard_map/reduce_scatter | solution.py:170
Sparse Core Ops, SparseCore 0:
  87.5 30.8 all-gather.1
  154.5 32.3 reduce-scatter.1

commit v2 on v1

--- a/solution.py
+++ b/solution.py
@@ -1,3 +1,4 @@
+import functools
 import math
 
 import jax
@@ -9,9 +10,6 @@
 
 HD = 128
 CH = 64
-NB = 2
-
-
 EPS = 1e-06
 SCALE = 1.0 / math.sqrt(HD)
 NT = (((1,), (1,)), ((), ()))
@@ -107,6 +105,339 @@
     )(e, wk, wv, q, go, qg.reshape(1, HD), kg.reshape(1, HD))
 
 
+MESH = pl.DeviceIdType.MESH
+NX, NZ, NT_DEV, NG = 4, 8, 4, 2
+SUB = 16
+PER = 8
+
+
+def place():
+    s = lax.axis_index("seq")
+    return s // NZ, s % NZ, lax.axis_index("tp"), lax.axis_index("grp")
+
+
+def at(x, z, t, g):
+    return (lax.rem(x + NX, NX) * NZ + lax.rem(z + NZ, NZ), lax.rem(t + NT_DEV, NT_DEV), lax.rem(g + NG, NG))
+
+
+X_PEERS = [(k, 0, 0, 0) for k in (1, 2, 3)]
+Z_PEERS = [(0, k, 0, 0) for k in (1, -1, 2, -2, 3, -3)]
+Y_PEERS = [(0, 0, t, g) for t in range(NT_DEV) for g in range(NG) if (t, g) != (0, 0)]
+META_PEERS = [(0, 1, 0, 1), (0, -1, 0, 1)]
+
+
+def greet(peers):
+    x, z, t, g = place()
+    barrier = pltpu.get_barrier_semaphore()
+    for dx, dz, dt, dg in peers:
+        pl.semaphore_signal(barrier, inc=1, device_id=at(x + dx, z + dz, t + dt, g + dg), device_id_type=MESH)
+
+
+def met(peers):
+    pl.semaphore_wait(pltpu.get_barrier_semaphore(), len(peers))
+
+
+def push(src, dst, send, recv, device):
+    pltpu.make_async_remote_copy(
+        src_ref=src, dst_ref=dst, send_sem=send, recv_sem=recv, device_id=device, device_id_type=MESH
+    ).start()
+
+
+def arrive(view, sem):
+    pltpu.make_async_copy(view, view, sem).wait()
+
+
+def choose(tiles, picks, index):
+    result = tiles[0]
+    for k in range(1, len(tiles)):
+        result = jnp.where(index == picks[k], tiles[k], result)
+    return result
+
+
+def dispatch_kernel(
+    chunks, t_ref, no_ref, nb_ref, e_ref, meta_ref,
+    perm, sent, xr, zb, mg, zr, fin, meta, mets,
+    x_s, x_r, z1_s, z1_r, z2_s, z2_r, y_s, y_r, m_s, m_r, m_l,
+):
+    x, z, t, g = place()
+    wide = nb_ref.shape[2] // chunks
+    peers = X_PEERS + Z_PEERS + Y_PEERS + META_PEERS
+    greet(peers)
+
+    lane = lax.broadcasted_iota(jnp.int32, (8, 128), 1)
+    row = jnp.zeros((8, 128), jnp.int32)
+    for p in range(PER):
+        owner = no_ref[0, p]
+        row = jnp.where(lane == p, owner, row)
+        row = jnp.where(lane == PER + owner, p, row)
+    meta[1 * NG + g] = row
+    size = t_ref.shape[1]
+    order = lax.broadcasted_iota(jnp.int32, (size, size), 0)
+    perm[...] = (order == t_ref[...]).astype(jnp.bfloat16)
+    met(peers)
+    mine = meta.at[NG + g]
+    push(mine, mine, m_s, m_r, at(x, z, t, g + 1))
+    for dg in range(NG):
+        push(mine, meta.at[g], m_s, m_r, at(x, z + 1, t, g + dg))
+        push(mine, meta.at[2 * NG + g], m_s, m_r, at(x, z - 1, t, g + dg))
+
+    def columns(c):
+        return pl.ds(pl.multiple_of(c * wide, wide), wide)
+
+    def stage_x(c):
+        rows = nb_ref[:, :, columns(c)].reshape(size, wide)
+        sent[c] = dot(perm[...], rows, NN).astype(jnp.bfloat16).reshape(NX, NZ, NG, SUB, wide)
+        for dx, _, _, _ in X_PEERS:
+            to = lax.rem(x + dx, NX)
+            push(sent.at[c, to], xr.at[c, :, :, x], x_s.at[c], x_r.at[c], at(to, z, t, g))
+        pltpu.make_async_copy(sent.at[c, x], xr.at[c, :, :, x], x_r.at[c]).start()
+
+    def stage_z1(c):
+        arrive(xr.at[c], x_r.at[c])
+        for way, sign in ((0, 1), (1, -1)):
+            for k in (3, 2, 1):
+                dest = lax.rem(z + sign * (k + 1) + NZ, NZ)
+                if k == 3:
+                    src, dst = xr.at[c, dest, way], zb.at[c, way, 4]
+                else:
+                    src, dst = xr.at[c, dest], zb.at[c, way, pl.ds(2 * (k - 1), 2)]
+                push(src, dst, z1_s.at[c], z1_r.at[c], at(x, z + sign * k, t, g))
+
+    def stage_z2(c):
+        arrive(zb.at[c], z1_r.at[c])
+        for way, sign in ((0, 1), (1, -1)):
+            dest = lax.rem(z + sign + NZ, NZ)
+            for h in range(NG):
+                far = 3 if h == way else 2
+                tiles = [xr[c, dest, h, xo] for xo in range(NX)]
+                for k in range(1, far + 1):
+                    part = 4 if k == 3 else 2 * (k - 1) + h
+                    tiles += [zb[c, way, part, xo] for xo in range(NX)]
+                for p in range(PER):
+                    owner = mets[(1 + sign) * NG + h, 0, p]
+                    rel = lax.rem(sign * (z - lax.rem(owner, NZ)) + NZ, NZ)
+                    mg[c, way, h, p] = choose(tiles, range(len(tiles)), rel * NX + owner // NZ)
+            push(mg.at[c, way], zr.at[c, way], z2_s.at[c], z2_r.at[c], at(x, z + sign, t, g))
+
+    def stage_y(c):
+        arrive(mg.at[c], z2_r.at[c])
+        for h in range(NG):
+            own = [xr[c, z, h, xo] for xo in range(NX)]
+            for p in range(PER):
+                owner = mets[NG + h, 0, p]
+                rel = lax.rem(z - lax.rem(owner, NZ) + NZ, NZ)
+                back = jnp.where(rel >= (5 if h == 0 else 4), zr[c, 1, h, p], zr[c, 0, h, p])
+                near = choose(own, range(NX), owner // NZ)
+                fin[c, h, p] = jnp.where(rel == 0, near, back)
+        slot = t * NG + g
+        for _, _, dt, dg in Y_PEERS:
+            to = lax.rem(g + dg, NG)
+            push(fin.at[c, to], e_ref.at[slot, :, :, columns(c)], y_s.at[c], y_r.at[c], at(x, z, t + dt, to))
+        pltpu.make_async_copy(fin.at[c, g], e_ref.at[slot, :, :, columns(c)], y_r.at[c]).start()
+
+    def step(i, carry):
+        @pl.when(i < chunks)
+        def _():
+            stage_x(i)
+
+        @pl.when((i >= 1) & (i <= chunks))
+        def _():
+            stage_z1(i - 1)
+
+        @pl.when(i == 1)
+        def _():
+            arrive(meta.at[pl.ds(0, 5)], m_r)
+            copy = pltpu.make_async_copy(meta, mets, m_l)
+            copy.start()
+            copy.wait()
+
+        @pl.when((i >= 2) & (i <= chunks + 1))
+        def _():
+            stage_z2(i - 2)
+
+        @pl.when(i >= 3)
+        def _():
+            stage_y(i - 3)
+        return carry
+    lax.fori_loop(0, chunks + 3, step, 0)
+
+    def drain(c, carry):
+        arrive(e_ref.at[:, :, :, columns(c)], y_r.at[c])
+        arrive(sent.at[c, pl.ds(0, 3)], x_s.at[c])
+        arrive(zb.at[c], z1_s.at[c])
+        arrive(mg.at[c], z2_s.at[c])
+        arrive(e_ref.at[pl.ds(0, 7), :, :, columns(c)], y_s.at[c])
+        return carry
+    lax.fori_loop(0, chunks, drain, 0)
+    arrive(meta.at[pl.ds(0, 5)], m_s)
+    meta_ref[...] = meta[...]
+
+
+def dispatch(chunks, t_row, owners, neighbours):
+    sub, slots, enc = neighbours.shape
+    wide = enc // chunks
+    vm = pl.BlockSpec(memory_space=pltpu.VMEM)
+    tile = (SUB, wide)
+    bf = jnp.bfloat16
+    dma = pltpu.SemaphoreType.DMA
+    return pl.pallas_call(
+        functools.partial(dispatch_kernel, chunks),
+        out_shape=(
+            jax.ShapeDtypeStruct((NT_DEV * NG, PER, SUB, enc), bf),
+            jax.ShapeDtypeStruct((3 * NG, 8, 128), jnp.int32),
+        ),
+        in_specs=[vm, pl.BlockSpec(memory_space=pltpu.SMEM), vm],
+        out_specs=(vm, vm),
+        scratch_shapes=[
+            pltpu.VMEM((sub * slots, sub * slots), bf),
+            pltpu.VMEM((chunks, NX, NZ, NG) + tile, bf),
+            pltpu.VMEM((chunks, NZ, NG, NX) + tile, bf),
+            pltpu.VMEM((chunks, 2, 5, NX) + tile, bf),
+            pltpu.VMEM((chunks, 2, NG, PER) + tile, bf),
+            pltpu.VMEM((chunks, 2, NG, PER) + tile, bf),
+            pltpu.VMEM((chunks, NG, PER) + tile, bf),
+            pltpu.VMEM((3 * NG, 8, 128), jnp.int32),
+            pltpu.SMEM((3 * NG, 8, 128), jnp.int32),
+        ] + [dma((chunks,))] * 8 + [dma, dma, dma],
+        name="dispatch",
+        compiler_params=pltpu.CompilerParams(
+            collective_id=0, has_side_effects=True, vmem_limit_bytes=56 * 2**20
+        ),
+    )(t_row, owners, neighbours)
+
+
+def return_kernel(
+    chunks, t_ref, mets, d_ref, out_ref,
+    perm, yr, gs, r1, fw, rz, fr,
+    y_s, y_r, r1_s, r1_r, r2_s, r2_r, x_s, x_r,
+):
+    x, z, t, g = place()
+    wide = out_ref.shape[2] // chunks
+    peers = X_PEERS + Z_PEERS + Y_PEERS
+    greet(peers)
+    size = t_ref.shape[0]
+    order = lax.broadcasted_iota(jnp.int32, (size, size), 1)
+    perm[...] = (order == t_ref[...]).astype(jnp.bfloat16)
+    met(peers)
+
+    def columns(c):
+        return pl.ds(pl.multiple_of(c * wide, wide), wide)
+
+    def stage_y(c):
+        slot = t * NG + g
+        for _, _, dt, dg in Y_PEERS:
+            tt, gg = lax.rem(t + dt, NT_DEV), lax.rem(g + dg, NG)
+            push(d_ref.at[tt * NG + gg, :, :, columns(c)], yr.at[c, slot], y_s.at[c], y_r.at[c], at(x, z, tt, gg))
+        pltpu.make_async_copy(d_ref.at[slot, :, :, columns(c)], yr.at[c, slot], y_r.at[c]).start()
+
+    def stage_r1(c):
+        arrive(yr.at[c], y_r.at[c])
+        for h in range(NG):
+            total = yr[c, h].astype(jnp.float32)
+            for k in range(1, NT_DEV):
+                total = total + yr[c, k * NG + h].astype(jnp.float32)
+            gs[c, h] = total.astype(jnp.bfloat16)
+        push(gs.at[c], r1.at[c, 0], r1_s.at[c], r1_r.at[c], at(x, z + 1, t, g))
+        push(gs.at[c], r1.at[c, 1], r1_s.at[c], r1_r.at[c], at(x, z - 1, t, g))
+
+    def select(tiles, near, h, row, xo):
+        position = mets[near * NG + h, 0, PER + xo * NZ + row]
+        return choose(tiles, range(PER), position)
+
+    def stage_r2(c):
+        arrive(r1.at[c], r1_r.at[c])
+        for way, sign in ((0, 1), (1, -1)):
+            near = 0 if way == 0 else 2
+            block = lax.rem(z - sign + NZ, NZ)
+            for h in range(NG):
+                far = 3 if h == way else 2
+                tiles = [r1[c, way, h, p] for p in range(PER)]
+                for k in range(far + 1):
+                    row = lax.rem(z + sign * k + NZ, NZ)
+                    part = 4 if k == 3 else 2 * (k - 1) + h
+                    for xo in range(NX):
+                        value = select(tiles, near, h, row, xo)
+                        if k == 0:
+                            rz[c, block, h, xo] = value
+                        else:
+                            fw[c, way, part, xo] = value
+            for k in (3, 2, 1):
+                if k == 3:
+                    src, dst = fw.at[c, way, 4], rz.at[c, block, way]
+                else:
+                    src, dst = fw.at[c, way, pl.ds(2 * (k - 1), 2)], rz.at[c, block]
+                push(src, dst, r2_s.at[c], r2_r.at[c], at(x, z + sign * k, t, g))
+        for h in range(NG):
+            tiles = [gs[c, h, p] for p in range(PER)]
+            for xo in range(NX):
+                rz[c, z, h, xo] = select(tiles, 1, h, z, xo)
+
+    def stage_x(c):
+        arrive(fw.at[c], r2_r.at[c])
+        for dx, _, _, _ in X_PEERS:
+            to = lax.rem(x + dx, NX)
+            push(rz.at[c, :, :, to], fr.at[c, x], x_s.at[c], x_r.at[c], at(to, z, t, g))
+        pltpu.make_async_copy(rz.at[c, :, :, x], fr.at[c, x], x_r.at[c]).start()
+
+    def stage_out(c):
+        arrive(fr.at[c], x_r.at[c])
+        rows = fr[c].reshape(size, wide)
+        placed = dot(perm[...], rows, NN).astype(jnp.bfloat16)
+        out_ref[:, :, columns(c)] = placed.reshape(out_ref.shape[0], out_ref.shape[1], wide)
+
+    def step(i, carry):
+        for k, stage in enumerate((stage_y, stage_r1, stage_r2, stage_x, stage_out)):
+            @pl.when((i >= k) & (i < chunks + k))
+            def _(stage=stage, k=k):
+                stage(i - k)
+        return carry
+    lax.fori_loop(0, chunks + 4, step, 0)
+
+    def drain(c, carry):
+        arrive(d_ref.at[pl.ds(0, 7), :, :, columns(c)], y_s.at[c])
+        arrive(r1.at[c], r1_s.at[c])
+        arrive(fw.at[c], r2_s.at[c])
+        arrive(fr.at[c, pl.ds(0, 3)], x_s.at[c])
+        return carry
+    lax.fori_loop(0, chunks, drain, 0)
+
+
+def give_back(chunks, t_col, mets, partial, slots):
+    groups, per, sub, enc = partial.shape
+    wide = enc // chunks
+    vm = pl.BlockSpec(memory_space=pltpu.VMEM)
+    tile = (SUB, wide)
+    bf = jnp.bfloat16
+    dma = pltpu.SemaphoreType.DMA
+    return pl.pallas_call(
+        functools.partial(return_kernel, chunks),
+        out_shape=jax.ShapeDtypeStruct((sub, slots, enc), bf),
+        in_specs=[vm, pl.BlockSpec(memory_space=pltpu.SMEM), vm],
+        out_specs=vm,
+        scratch_shapes=[
+            pltpu.VMEM((sub * slots, sub * slots), bf),
+            pltpu.VMEM((chunks, NT_DEV * NG, PER) + tile, bf),
+            pltpu.VMEM((chunks, NG, PER) + tile, bf),
+            pltpu.VMEM((chunks, 2, NG, PER) + tile, bf),
+            pltpu.VMEM((chunks, 2, 5, NX) + tile, bf),
+            pltpu.VMEM((chunks, NZ, NG, NX) + tile, bf),
+            pltpu.VMEM((chunks, NX, NZ, NG) + tile, bf),
+        ] + [dma((chunks,))] * 8,
+        name="give_back",
+        compiler_params=pltpu.CompilerParams(
+            collective_id=1, has_side_effects=True, vmem_limit_bytes=56 * 2**20
+        ),
+    )(t_col, mets, partial)
+
+
+def targets(owner_slots):
+    block = jnp.where(owner_slots >= 0, owner_slots // PER, -SUB) * SUB
+    return (block[None, :] + jnp.arange(SUB, dtype=jnp.int32)[:, None]).reshape(-1)
+
+
+CHUNKS = 8
+
+
 def shards(
     queries,
     out_grad,
@@ -118,73 +449,12 @@
     neighbour_owner,
     owner_slots,
 ):
-    tok_rows, col_width = queries.shape
-    stretches_dev = tok_rows // CH
-    per_dev = stretches_dev * NB
-    seq_count = lax.axis_size("seq")
-    grp_count = lax.axis_size("grp")
-    slot_count = owner_slots.shape[0]
-    pair_cap = slot_count // (grp_count * seq_count)
-    slot_span = seq_count * pair_cap
-    rows_own = neighbours.shape[0]
-    rows_tp = rows_own * grp_count
-    enc_width = neighbours.shape[2]
-    occupied = owner_slots >= 0
-    target_dev = jnp.where(occupied, owner_slots // NB // stretches_dev, -1)
-    dest_seq = target_dev // grp_count
-    dest_grp = target_dev % grp_count
-    slot_order = jnp.arange(slot_count, dtype=jnp.int32)
-    same_dest = (target_dev[:, None] == target_dev[None, :]) & (
-        owner_slots[None, :] < owner_slots[:, None]
-    )
-    pair_rank = jnp.sum(same_dest.astype(jnp.int32), axis=1)
-    target = jnp.where(occupied, dest_grp * slot_span + dest_seq * pair_cap + pair_rank, -1)
-    chooser = (
-        (slot_order[:, None] == target[None, :])
-        .astype(jnp.bfloat16)
-        .reshape(grp_count, slot_span, slot_count)
-    )
-    outgoing = jnp.einsum(
-        "gqs,rsd->rgqd", chooser, neighbours, preferred_element_type=jnp.float32
-    ).astype(jnp.bfloat16)
-    arrived = lax.all_to_all(
-        lax.all_to_all(outgoing, "seq", split_axis=2, concat_axis=2, tiled=True),
-        "grp",
-        split_axis=1,
-        concat_axis=0,
-        tiled=True,
-    )
-    arrived = arrived.reshape(rows_tp, slot_span, enc_width)
-    owners = neighbour_owner.reshape(-1)
-    positions = jnp.arange(per_dev, dtype=jnp.int32)
-    earlier = (owners[:, None] == owners[None, :]) & (positions[None, :] < positions[:, None])
-    picked = owners * pair_cap + jnp.sum(earlier.astype(jnp.int32), axis=1)
-    used_rows = jnp.take(arrived, picked, axis=1)
-    shard_piece = lax.all_gather(used_rows, "tp", axis=0, tiled=True)
-    groups = shard_piece.shape[0] // 16
-    enc = shard_piece.reshape(groups, 16, per_dev, enc_width).transpose(0, 2, 1, 3)
-    query_grad, enc_grad = compute(
+    target = targets(owner_slots)
+    enc, meta = dispatch(CHUNKS, target.reshape(1, -1), neighbour_owner.reshape(1, -1), neighbours)
+    query_grad, partial = compute(
         enc, key_weight, value_weight, queries, out_grad, query_gain, key_gain
     )
-    term_rows = enc_grad.transpose(0, 2, 1, 3)
-    summed = lax.psum_scatter(
-        term_rows.reshape(lax.axis_size("tp") * rows_tp, per_dev, enc_width),
-        "tp",
-        scatter_dimension=0,
-        tiled=True,
-    )
-    outbound = jnp.zeros((rows_tp, slot_span, enc_width), jnp.bfloat16).at[:, picked].set(summed)
-    outbound = outbound.reshape(rows_tp, 1, slot_span, enc_width)
-    returned = lax.all_to_all(
-        lax.all_to_all(outbound, "seq", split_axis=2, concat_axis=2, tiled=True),
-        "grp",
-        split_axis=0,
-        concat_axis=1,
-        tiled=True,
-    )
-    neighbour_grad = jnp.einsum(
-        "gqs,rgqd->rsd", chooser, returned, preferred_element_type=jnp.float32
-    ).astype(jnp.bfloat16)
+    neighbour_grad = give_back(CHUNKS, target.reshape(-1, 1), meta, partial, owner_slots.shape[0])
     return (query_grad, neighbour_grad)
 
 

time: 270 us -> 160 us (0.59)
  Pallas kernels: 28.5 us -> 152 us
  waiting for transfers between devices: 112 us -> 0 us
  blocking collectives: 73.8 us -> 0 us
  local copies, waits for them, and re-layouts: 22.1 us -> 6.44 us
  between operations: 14.1 us -> 0.65 us
  starting transfers between devices: 12.2 us -> 0 us
  matrix products: 2.97 us -> 0 us
  other arithmetic: 3.55 us -> 0.67 us
    pallas_call x0 -> x2, Pallas kernels: none -> 124 us  [the longest x1 66.6 us: dispatch(): pl.pallas_call(functools.partial(dispatch_kernel, chunks), out_shape=(jax...]
    all_to_all x3 -> x0, blocking collectives: 73.8 us -> none  [the longest x1 56.6 us: shards(): lax.all_to_all(outbound, 'seq', split_axis=2, concat_axis=2, tiled=True)]
    all_to_all x1 -> x0, waiting for transfers between devices: 48.3 us -> none  [shards(): lax.all_to_all(outgoing, 'seq', split_axis=2, concat_axis=2, tiled=True)]
    reduce_scatter x1 -> x0, waiting for transfers between devices: 32.5 us -> none  [shards(): lax.psum_scatter(term_rows.reshape(lax.axis_size('tp') * rows_tp, per_dev...]
    all_gather x1 -> x0, waiting for transfers between devices: 31 us -> none  [shards(): shard_piece = lax.all_gather(used_rows, 'tp', axis=0, tiled=True)]
    all_to_all x1 -> x0, starting transfers between devices: 12.1 us -> none  [shards(): lax.all_to_all(outgoing, 'seq', split_axis=2, concat_axis=2, tiled=True)]
    all_to_all x3 -> x0, local copies, waits for them, and re-layouts: 4.4 us -> none  [the longest x1 1.76 us: shards(): lax.all_to_all(outgoing, 'seq', split_axis=2, concat_axis=2, tiled=True)]
    transpose x1 -> x0, local copies, waits for them, and re-layouts: 4.19 us -> none  [shards(): term_rows = enc_grad.transpose(0, 2, 1, 3)]
  transfers between devices with their start and end apart: 3 -> 0, of which waited for: 3 -> 0; matrix products, arithmetic and copies ran while one was open for 0% -> 0% of each run, Pallas kernels for 0% -> 0%
where the time goes in v2:
time: 160 us
  Pallas kernels  152 us (95%)
  local copies, waits for them, and re-layouts  6.44 us (4%)
    pallas_call x1, Pallas kernels, dispatch(): pl.pallas_call(functools.partial(dispatch_kernel, chunks), out_shape=(jax...  66.6 us
    pallas_call x1, Pallas kernels, give_back(): pl.pallas_call(functools.partial(return_kernel, chunks), out_shape=jax.Sh...  57.4 us
    pallas_call x1, Pallas kernels, compute(): pl.pallas_call(compute_kernel, out_shape=(jax.ShapeDtypeStruct(q.shape, j...  28.5 us
    unnamed x2, local copies, waits for them, and re-layouts  3.91 us

profile of v2, /device:TPU:1, one launch (start us, length us, event | category | flops | bytes accessed | tf_op | source)
XLA Modules:
  0.0 160.3 jit_solution(3250036417680342579)
XLA Ops:
  0.6 0.7 fusion
  1.3 0.7 add.37.t_ref
  2.0 0.8 copy.12
  2.7 0.6 reshape.58.no_ref
  3.3 66.6 %dispatch.1 = (bf16[8,8,16,1024]{3,2,1,0:T(8,128)(2,1)}, s32[6,8,128]{2,1,0:T(8,128)}) custom-call(s32[1,1024]{1,0:T(1,128)} %add.37.t_ref, s32[1,8]{1,0:T(1,128)} %reshape.58.no_ref, bf16[16,64,1024]{2,1,0:T(8,128)(2,1)} %nb_ref.1), custom_call_target="tpu_custom_call" | custom-call | tf_op jit(solution)/shard_map/dispatch/pallas_call | solution.py:283
  69.9 28.5 %attention.1 = (bf16[256,1024]{1,0:T(8,128)(2,1)}, bf16[8,8,16,1024]{3,2,1,0:T(8,128)(2,1)}) custom-call(bf16[8,8,16,1024]{3,2,1,0:T(8,128)(2,1)} %get-tuple-element.6.e_ref, bf16[1024,1024]{1,0:T(8,128)(2,1)} %wk_ref.1, bf16[1024,1024]{1,0:T(8,128)(2,1)} %wv_ref.1, bf16[256,1024]{1,0:T(8,128)(2,1)} %q_ref.1, bf16[256,1024]{1,0:T(8,128)(2,1)} %go_ref.1, ...), custom_call_target="tpu_custom_call" | custom-call | tf_op jit(solution)/shard_map/attention/pallas_call | solution.py:97
  98.4 1.3 add.39.t_ref
  99.7 57.4 %give_back.1 = bf16[16,64,1024]{2,1,0:T(8,128)(2,1)} custom-call(s32[1024,1]{1,0:T(8,128)} %add.39.t_ref, s32[6,8,128]{2,1,0:T(8,128)} %get-tuple-element.8.mets, bf16[8,8,16,1024]{3,2,1,0:T(8,128)(2,1)} %get-tuple-element.9.d_ref), custom_call_target="tpu_custom_call" | custom-call | tf_op jit(solution)/shard_map/give_back/pallas_call | solution.py:412
  157.1 3.1 %copy.15 = bf16[16,64,1024]{2,1,0:T(8,128)(2,1)} copy(bf16[16,64,1024]{2,1,0:T(8,128)(2,1)} %give_back.1) | data formatting | bytes 4194304
  (1 shorter events, 0.0 us)

commit v3 on v1

v3 whole, which is shorter than its diff:
```python
import functools
import math

import jax
import jax.numpy as jnp
from jax import lax
from jax.experimental import pallas as pl
from jax.experimental.pallas import tpu as pltpu
from jax.sharding import PartitionSpec as P

HD = 128
CH = 64
EPS = 1e-06
SCALE = 1.0 / math.sqrt(HD)
NT = (((1,), (1,)), ((), ()))
TN = (((0,), (0,)), ((), ()))
NN = (((1,), (0,)), ((), ()))
MESH = pl.DeviceIdType.MESH
NX, NZ, NT_DEV, NG = 4, 8, 4, 2
SUB = 16
PER = 8
CHUNKS = 8


def dot(a, b, dims):
    return lax.dot_general(a, b, dims, preferred_element_type=jnp.float32)


def place():
    s = lax.axis_index("seq")
    return s // NZ, s % NZ, lax.axis_index("tp"), lax.axis_index("grp")


def at(x, z, t, g):
    return (lax.rem(x + NX, NX) * NZ + lax.rem(z + NZ, NZ), lax.rem(t + NT_DEV, NT_DEV), lax.rem(g + NG, NG))


X_PEERS = [(k, 0, 0, 0) for k in (1, 2, 3)]
Z_PEERS = [(0, k, 0, 0) for k in (1, -1, 2, -2, 3, -3)]
Y_PEERS = [(0, 0, t, g) for t in range(NT_DEV) for g in range(NG) if (t, g) != (0, 0)]
META_PEERS = [(0, 1, 0, 1), (0, -1, 0, 1)]


def greet(peers):
    x, z, t, g = place()
    barrier = pltpu.get_barrier_semaphore()
    for dx, dz, dt, dg in peers:
        pl.semaphore_signal(barrier, inc=1, device_id=at(x + dx, z + dz, t + dt, g + dg), device_id_type=MESH)


def met(peers):
    pl.semaphore_wait(pltpu.get_barrier_semaphore(), len(peers))


def push(src, dst, send, recv, device):
    pltpu.make_async_remote_copy(
        src_ref=src, dst_ref=dst, send_sem=send, recv_sem=recv, device_id=device, device_id_type=MESH
    ).start()


def arrive(view, sem):
    pltpu.make_async_copy(view, view, sem).wait()


def choose(tiles, picks, index):
    result = tiles[0]
    for k in range(1, len(tiles)):
        result = jnp.where(index == picks[k], tiles[k], result)
    return result


def attend(e_ref, kacc, vacc, wk_ref, wv_ref, q_ref, go_ref, qg_ref, kg_ref, qgrad_ref, dkr_ref, dv_ref):
    rows, width = q_ref.shape
    stretches = rows // CH
    groups, per_dev, sub, enc = e_ref.shape
    keys = groups * 2 * sub
    qgain = qg_ref[...]
    kgain = kg_ref[...]

    def pair(i, carry):
        cols = pl.ds(pl.multiple_of(i * 2 * HD, 2 * HD), 2 * HD)
        last = slice(enc - 256, enc)
        enc_rows = e_ref[:, :, :, last].reshape(groups * per_dev * sub, 256)
        kr2 = kacc[:, cols] + dot(enc_rows, wk_ref[last, cols], NN)
        val2 = (vacc[:, cols] + dot(enc_rows, wv_ref[last, cols], NN)).astype(jnp.bfloat16)
        for hh in range(2):
            lanes = slice(hh * HD, (hh + 1) * HD)
            head = pl.ds(pl.multiple_of((i * 2 + hh) * HD, HD), HD)
            kr = kr2[:, lanes]
            val = val2[:, lanes].reshape(groups, per_dev, sub, HD)
            kinv = lax.rsqrt(jnp.mean(kr * kr, axis=-1, keepdims=True) + EPS)
            khat = kr * kinv
            kn = (khat * kgain).astype(jnp.bfloat16).reshape(groups, per_dev, sub, HD)
            khat = khat.reshape(groups, per_dev, sub, HD)
            kinv = kinv.reshape(groups, per_dev, sub, 1)
            qx = q_ref[:, head].astype(jnp.float32)
            qinv = lax.rsqrt(jnp.mean(qx * qx, axis=-1, keepdims=True) + EPS)
            qhat = qx * qinv
            qn = (qhat * qgain).astype(jnp.bfloat16)
            go = go_ref[:, head]
            for c in range(stretches):
                tok = slice(c * CH, (c + 1) * CH)
                kn_c = kn[:, 2 * c:2 * c + 2].reshape(keys, HD)
                val_c = val[:, 2 * c:2 * c + 2].reshape(keys, HD)
                qn_c, go_c = qn[tok], go[tok]
                weights = jnp.exp(dot(qn_c, kn_c, NT) * SCALE)
                prob = weights * (1.0 / jnp.sum(weights, axis=-1, keepdims=True))
                dp = dot(go_c, val_c, NT)
                inner = jnp.sum(prob * dp, axis=-1, keepdims=True)
                ds = (prob * (dp - inner)).astype(jnp.bfloat16)
                pb = prob.astype(jnp.bfloat16)
                dv_c = dot(pb, go_c, TN).astype(jnp.bfloat16)
                dkn = dot(ds, qn_c, TN)
                dqn = dot(ds, kn_c, NN)
                qs = dqn * (qgain * SCALE)
                qh = qhat[tok]
                qi = jnp.mean(qh * qs, axis=-1, keepdims=True)
                qgrad_ref[tok, head] = (qinv[tok] * (qs - qh * qi)).astype(jnp.bfloat16)
                ks = dkn * (kgain * SCALE)
                kh = khat[:, 2 * c:2 * c + 2].reshape(keys, HD)
                ki = jnp.mean(kh * ks, axis=-1, keepdims=True)
                kv = kinv[:, 2 * c:2 * c + 2].reshape(keys, 1)
                dk = (kv * (ks - kh * ki)).astype(jnp.bfloat16)
                dkr_ref[:, 2 * c:2 * c + 2, :, head] = dk.reshape(groups, 2, sub, HD)
                dv_ref[:, 2 * c:2 * c + 2, :, head] = dv_c.reshape(groups, 2, sub, HD)
        return carry
    lax.fori_loop(0, width // (2 * HD), pair, 0)


def kernel(
    slots_ref, no_ref, qg_ref, kg_ref, nb_hbm, wk_hbm, wv_hbm, q_hbm, go_hbm,
    qgrad_hbm, out_hbm,
    nb, wk, wv, q, go, qgrad, perm, perm_back,
    sent, xr, zb, mg, zr, fin, enc, kacc, vacc, dkr, dv,
    part, yr, gs, r1, fw, rz, fr, placed_ref, meta, mets,
    x_s, x_r, z1_s, z1_r, z2_s, z2_r, y_s, y_r,
    by_s, by_r, r1_s, r1_r, r2_s, r2_r, bx_s, bx_r, out_sem,
    m_s, m_r, m_l, in_sem, q_sem,
):
    x, z, t, g = place()
    chunks = CHUNKS
    wide = nb.shape[2] // chunks
    slots = nb.shape[1]
    size = SUB * slots
    peers = X_PEERS + Z_PEERS + Y_PEERS + META_PEERS
    greet(peers)
    loads = [
        pltpu.make_async_copy(src, dst, in_sem.at[k])
        for k, (src, dst) in enumerate(((nb_hbm, nb), (wk_hbm, wk), (wv_hbm, wv), (q_hbm, q), (go_hbm, go)))
    ]
    for load in loads:
        load.start()

    lane8 = lax.broadcasted_iota(jnp.int32, (8, 128), 1)
    row = jnp.zeros((8, 128), jnp.int32)
    for p in range(PER):
        owner = no_ref[p // 2, p % 2]
        row = jnp.where(lane8 == p, owner, row)
        row = jnp.where(lane8 == PER + owner, p, row)
    meta[1 * NG + g] = row

    def block(s):
        number = slots_ref[s]
        return jnp.where(number >= 0, number // PER, -SUB) * SUB

    lane = lax.broadcasted_iota(jnp.int32, (1, 128), 1)
    base = jnp.zeros((1, 128), jnp.int32)
    for s in range(slots):
        base = jnp.where(lax.rem(lane, slots) == s, block(s), base)
    base = base + lane // slots
    order = lax.broadcasted_iota(jnp.int32, (size, 128), 0)
    for k in range(size // 128):
        perm[:, k * 128:(k + 1) * 128] = (order == base + k * (128 // slots)).astype(jnp.bfloat16)
    met(peers)
    mine = meta.at[NG + g]
    push(mine, mine, m_s, m_r, at(x, z, t, g + 1))
    for dg in range(NG):
        push(mine, meta.at[g], m_s, m_r, at(x, z + 1, t, g + dg))
        push(mine, meta.at[2 * NG + g], m_s, m_r, at(x, z - 1, t, g + dg))
    loads[0].wait()

    def columns(c):
        return pl.ds(pl.multiple_of(c * wide, wide), wide)

    def stage_x(c):
        rows = nb[:, :, columns(c)].reshape(size, wide)
        sent[c] = dot(perm[...], rows, NN).astype(jnp.bfloat16).reshape(NX, NZ, NG, SUB, wide)
        for dx, _, _, _ in X_PEERS:
            to = lax.rem(x + dx, NX)
            push(sent.at[c, to], xr.at[c, :, :, x], x_s.at[c], x_r.at[c], at(to, z, t, g))
        pltpu.make_async_copy(sent.at[c, x], xr.at[c, :, :, x], x_r.at[c]).start()

    def stage_z1(c):
        arrive(xr.at[c], x_r.at[c])
        for way, sign in ((0, 1), (1, -1)):
            for k in (3, 2, 1):
                dest = lax.rem(z + sign * (k + 1) + NZ, NZ)
                if k == 3:
                    src, dst = xr.at[c, dest, way], zb.at[c, way, 4]
                else:
                    src, dst = xr.at[c, dest], zb.at[c, way, pl.ds(2 * (k - 1), 2)]
                push(src, dst, z1_s.at[c], z1_r.at[c], at(x, z + sign * k, t, g))

    def stage_z2(c):
        arrive(zb.at[c], z1_r.at[c])
        for way, sign in ((0, 1), (1, -1)):
            dest = lax.rem(z + sign + NZ, NZ)
            for h in range(NG):
                far = 3 if h == way else 2
                tiles = [xr[c, dest, h, xo] for xo in range(NX)]
                for k in range(1, far + 1):
                    part = 4 if k == 3 else 2 * (k - 1) + h
                    tiles += [zb[c, way, part, xo] for xo in range(NX)]
                for p in range(PER):
                    owner = mets[(1 + sign) * NG + h, 0, p]
                    rel = lax.rem(sign * (z - lax.rem(owner, NZ)) + NZ, NZ)
                    mg[c, way, h, p] = choose(tiles, range(len(tiles)), rel * NX + owner // NZ)
            push(mg.at[c, way], zr.at[c, way], z2_s.at[c], z2_r.at[c], at(x, z + sign, t, g))

    def stage_y(c):
        arrive(mg.at[c], z2_r.at[c])
        for h in range(NG):
            own = [xr[c, z, h, xo] for xo in range(NX)]
            for p in range(PER):
                owner = mets[NG + h, 0, p]
                rel = lax.rem(z - lax.rem(owner, NZ) + NZ, NZ)
                back = jnp.where(rel >= (5 if h == 0 else 4), zr[c, 1, h, p], zr[c, 0, h, p])
                near = choose(own, range(NX), owner // NZ)
                fin[c, h, p] = jnp.where(rel == 0, near, back)
        slot = t * NG + g
        for _, _, dt, dg in Y_PEERS:
            to = lax.rem(g + dg, NG)
            push(fin.at[c, to], enc.at[slot, :, :, columns(c)], y_s.at[c], y_r.at[c], at(x, z, t + dt, to))
        pltpu.make_async_copy(fin.at[c, g], enc.at[slot, :, :, columns(c)], y_r.at[c]).start()

    def project(j):
        rows = pl.ds(pl.multiple_of(j * 256, 256), 256)
        left = enc[:, :, :, rows].reshape(size, 256)

        def block_of(k, carry):
            cols = pl.ds(pl.multiple_of(k * 256, 256), 256)
            for acc, weight in ((kacc, wk), (vacc, wv)):
                term = dot(left, weight[rows, cols], NN)

                @pl.when(j == 0)
                def _(acc=acc, term=term):
                    acc[:, cols] = term

                @pl.when(j > 0)
                def _(acc=acc, term=term):
                    acc[:, cols] += term
            return carry
        lax.fori_loop(0, wk.shape[1] // 256, block_of, 0)

    def stage_p(c):
        arrive(enc.at[:, :, :, columns(c)], y_r.at[c])

        @pl.when(c == 0)
        def _():
            for load in loads[1:]:
                load.wait()

        @pl.when((lax.rem(c, 2) == 1) & (c < chunks - 1))
        def _():
            project(c // 2)

    def step(i, carry):
        @pl.when(i < chunks)
        def _():
            stage_x(i)

        @pl.when((i >= 1) & (i <= chunks))
        def _():
            stage_z1(i - 1)

        @pl.when(i == 1)
        def _():
            arrive(meta.at[pl.ds(0, 5)], m_r)
            copy = pltpu.make_async_copy(meta, mets, m_l)
            copy.start()
            copy.wait()

        @pl.when((i >= 2) & (i <= chunks + 1))
        def _():
            stage_z2(i - 2)

        @pl.when((i >= 3) & (i <= chunks + 2))
        def _():
            stage_y(i - 3)

        @pl.when(i >= 4)
        def _():
            stage_p(i - 4)
        return carry
    lax.fori_loop(0, chunks + 4, step, 0)

    attend(enc, kacc, vacc, wk, wv, q, go, qg_ref, kg_ref, qgrad, dkr, dv)
    give = pltpu.make_async_copy(qgrad, qgrad_hbm, q_sem)
    give.start()

    def back_y(c):
        slot = t * NG + g
        rows = columns(c)
        total = dot(dkr[...].reshape(size, -1), wk[rows, :], NT)
        total = total + dot(dv[...].reshape(size, -1), wv[rows, :], NT)
        part[c] = total.astype(jnp.bfloat16).reshape(NT_DEV * NG, PER, SUB, wide)
        for _, _, dt, dg in Y_PEERS:
            tt, gg = lax.rem(t + dt, NT_DEV), lax.rem(g + dg, NG)
            push(part.at[c, tt * NG + gg], yr.at[c, slot], by_s.at[c], by_r.at[c], at(x, z, tt, gg))
        pltpu.make_async_copy(part.at[c, slot], yr.at[c, slot], by_r.at[c]).start()

    def back_r1(c):
        arrive(yr.at[c], by_r.at[c])
        for h in range(NG):
            total = yr[c, h].astype(jnp.float32)
            for k in range(1, NT_DEV):
                total = total + yr[c, k * NG + h].astype(jnp.float32)
            gs[c, h] = total.astype(jnp.bfloat16)
        push(gs.at[c], r1.at[c, 0], r1_s.at[c], r1_r.at[c], at(x, z + 1, t, g))
        push(gs.at[c], r1.at[c, 1], r1_s.at[c], r1_r.at[c], at(x, z - 1, t, g))

    def select(tiles, near, h, row, xo):
        position = mets[near * NG + h, 0, PER + xo * NZ + row]
        return choose(tiles, range(PER), position)

    def back_r2(c):
        arrive(r1.at[c], r1_r.at[c])
        for way, sign in ((0, 1), (1, -1)):
            near = 0 if way == 0 else 2
            block = lax.rem(z - sign + NZ, NZ)
            for h in range(NG):
                far = 3 if h == way else 2
                tiles = [r1[c, way, h, p] for p in range(PER)]
                for k in range(far + 1):
                    row = lax.rem(z + sign * k + NZ, NZ)
                    part = 4 if k == 3 else 2 * (k - 1) + h
                    for xo in range(NX):
                        value = select(tiles, near, h, row, xo)
                        if k == 0:
                            rz[c, block, h, xo] = value
                        else:
                            fw[c, way, part, xo] = value
            for k in (3, 2, 1):
                if k == 3:
                    src, dst = fw.at[c, way, 4], rz.at[c, block, way]
                else:
                    src, dst = fw.at[c, way, pl.ds(2 * (k - 1), 2)], rz.at[c, block]
                push(src, dst, r2_s.at[c], r2_r.at[c], at(x, z + sign * k, t, g))
        for h in range(NG):
            tiles = [gs[c, h, p] for p in range(PER)]
            for xo in range(NX):
                rz[c, z, h, xo] = select(tiles, 1, h, z, xo)

    def back_x(c):
        arrive(fw.at[c], r2_r.at[c])
        for dx, _, _, _ in X_PEERS:
            to = lax.rem(x + dx, NX)
            push(rz.at[c, :, :, to], fr.at[c, x], bx_s.at[c], bx_r.at[c], at(to, z, t, g))
        pltpu.make_async_copy(rz.at[c, :, :, x], fr.at[c, x], bx_r.at[c]).start()

    def back_out(c):
        arrive(fr.at[c], bx_r.at[c])
        rows = fr[c].reshape(size, wide)
        placed = dot(perm_back[...], rows, NN).astype(jnp.bfloat16)
        placed_ref[c] = placed.reshape(SUB, slots, wide)
        pltpu.make_async_copy(placed_ref.at[c], out_hbm.at[:, :, columns(c)], out_sem.at[c]).start()

    def back_step(i, carry):
        for k, stage in enumerate((back_y, back_r1, back_r2, back_x, back_out)):
            @pl.when((i >= k) & (i < chunks + k))
            def _(stage=stage, k=k):
                stage(i - k)

        @pl.when(i == 0)
        def _():
            order = lax.broadcasted_iota(jnp.int32, (size, 128), 1)
            down = lax.broadcasted_iota(jnp.int32, (8, 128), 0)
            parts = []
            for k in range(slots // 8):
                value = jnp.zeros((8, 128), jnp.int32)
                for s in range(8):
                    value = jnp.where(down == s, block(k * 8 + s), value)
                parts.append(value)
            rows = jnp.concatenate(parts, axis=0)
            rows = jnp.concatenate([rows + r for r in range(SUB)], axis=0)
            for k in range(size // 128):
                perm_back[:, k * 128:(k + 1) * 128] = (order + k * 128 == rows).astype(jnp.bfloat16)
        return carry
    lax.fori_loop(0, chunks + 4, back_step, 0)

    def drain(c, carry):
        arrive(sent.at[c, pl.ds(0, 3)], x_s.at[c])
        arrive(zb.at[c], z1_s.at[c])
        arrive(mg.at[c], z2_s.at[c])
        arrive(part.at[c, pl.ds(0, 7)], y_s.at[c])
        arrive(part.at[c, pl.ds(0, 7)], by_s.at[c])
        arrive(r1.at[c], r1_s.at[c])
        arrive(fw.at[c], r2_s.at[c])
        arrive(fr.at[c, pl.ds(0, 3)], bx_s.at[c])
        pltpu.make_async_copy(placed_ref.at[c], out_hbm.at[:, :, columns(c)], out_sem.at[c]).wait()
        return carry
    lax.fori_loop(0, chunks, drain, 0)
    arrive(meta.at[pl.ds(0, 5)], m_s)
    give.wait()


def shards(
    queries,
    out_grad,
    query_gain,
    key_gain,
    key_weight,
    value_weight,
    neighbours,
    neighbour_owner,
    owner_slots,
):
    tokens, width = queries.shape
    sub, slots, deep = neighbours.shape
    bf = jnp.bfloat16
    f32 = jnp.float32
    size = sub * slots
    end = (SUB, deep // CHUNKS)
    rows = (NT_DEV * NG, PER, SUB, deep)
    vm = pl.BlockSpec(memory_space=pltpu.VMEM)
    sm = pl.BlockSpec(memory_space=pltpu.SMEM)
    hbm = pl.BlockSpec(memory_space=pl.ANY)
    dma = pltpu.SemaphoreType.DMA

    def tiles(*lead):
        return pltpu.VMEM((CHUNKS,) + lead + end, bf)
    scratch = [
        pltpu.VMEM(neighbours.shape, bf),
        pltpu.VMEM(key_weight.shape, bf),
        pltpu.VMEM(value_weight.shape, bf),
        pltpu.VMEM(queries.shape, bf),
        pltpu.VMEM(out_grad.shape, bf),
        pltpu.VMEM(queries.shape, bf),
        pltpu.VMEM((size, size), bf),
        pltpu.VMEM((size, size), bf),
        tiles(NX, NZ, NG),
        tiles(NZ, NG, NX),
        tiles(2, 5, NX),
        tiles(2, NG, PER),
        tiles(2, NG, PER),
        tiles(NG, PER),
        pltpu.VMEM(rows, bf),
        pltpu.VMEM((size, width), f32),
        pltpu.VMEM((size, width), f32),
        pltpu.VMEM(rows[:3] + (width,), bf),
        pltpu.VMEM(rows[:3] + (width,), bf),
        tiles(NT_DEV * NG, PER),
        tiles(NT_DEV * NG, PER),
        tiles(NG, PER),
        tiles(2, NG, PER),
        tiles(2, 5, NX),
        tiles(NZ, NG, NX),
        tiles(NX, NZ, NG),
        pltpu.VMEM((CHUNKS, sub, slots, deep // CHUNKS), bf),
        pltpu.VMEM((3 * NG, 8, 128), jnp.int32),
        pltpu.SMEM((3 * NG, 8, 128), jnp.int32),
    ]
    scratch += [dma((CHUNKS,))] * 17 + [dma, dma, dma, dma((5,)), dma]
    return pl.pallas_call(
        kernel,
        out_shape=(
            jax.ShapeDtypeStruct(queries.shape, bf),
            jax.ShapeDtypeStruct(neighbours.shape, bf),
        ),
        in_specs=[sm, sm, vm, vm] + [hbm] * 5,
        out_specs=(hbm, hbm),
        scratch_shapes=scratch,
        name="cross_attention_back",
        compiler_params=pltpu.CompilerParams(
            collective_id=0, has_side_effects=True, vmem_limit_bytes=60 * 2**20
        ),
    )(
        owner_slots, neighbour_owner, query_gain.reshape(1, HD), key_gain.reshape(1, HD),
        neighbours, key_weight, value_weight, queries, out_grad,
    )


def solution(mesh):
    in_specs = (
        P(("seq", "grp"), "tp"),
        P(("seq", "grp"), "tp"),
        P(),
        P(),
        P(None, "tp"),
        P(None, "tp"),
        P(("tp", "grp"), "seq", None),
        P(("seq", "grp"), None),
        P("seq"),
    )
    out_specs = (P(("seq", "grp"), "tp"), P(("tp", "grp"), "seq", None))
    return jax.shard_map(shards, mesh=mesh, in_specs=in_specs, out_specs=out_specs, check_vma=False)
```

time: 270 us -> 151 us (0.56)
  Pallas kernels: 28.5 us -> 144 us
  waiting for transfers between devices: 112 us -> 0 us
  blocking collectives: 73.8 us -> 0 us
  local copies, waits for them, and re-layouts: 22.1 us -> 6.35 us
  between operations: 14.1 us -> 0.64 us
  starting transfers between devices: 12.2 us -> 0 us
  other arithmetic: 3.55 us -> 0 us
  matrix products: 2.97 us -> 0 us
    pallas_call x1, Pallas kernels: 28.5 us -> 144 us  [shards(): pl.pallas_call(kernel, out_shape=(jax.ShapeDtypeStruct(queries.shape, bf)...]
    all_to_all x3 -> x0, blocking collectives: 73.8 us -> none  [the longest x1 56.6 us: shards(): lax.all_to_all(outbound, 'seq', split_axis=2, concat_axis=2, tiled=True)]
    all_to_all x1 -> x0, waiting for transfers between devices: 48.3 us -> none  [shards(): lax.all_to_all(outgoing, 'seq', split_axis=2, concat_axis=2, tiled=True)]
    reduce_scatter x1 -> x0, waiting for transfers between devices: 32.5 us -> none  [shards(): lax.psum_scatter(term_rows.reshape(lax.axis_size('tp') * rows_tp, per_dev...]
    all_gather x1 -> x0, waiting for transfers between devices: 31 us -> none  [shards(): shard_piece = lax.all_gather(used_rows, 'tp', axis=0, tiled=True)]
    all_to_all x1 -> x0, starting transfers between devices: 12.1 us -> none  [shards(): lax.all_to_all(outgoing, 'seq', split_axis=2, concat_axis=2, tiled=True)]
    unnamed x5 -> x3, local copies, waits for them, and re-layouts: 0.11 us -> 6.35 us
    all_to_all x3 -> x0, local copies, waits for them, and re-layouts: 4.4 us -> none  [the longest x1 1.76 us: shards(): lax.all_to_all(outgoing, 'seq', split_axis=2, concat_axis=2, tiled=True)]
  transfers between devices with their start and end apart: 3 -> 0, of which waited for: 3 -> 0; matrix products, arithmetic and copies ran while one was open for 0% -> 0% of each run, Pallas kernels for 0% -> 0%
where the time goes in v3:
time: 151 us
  Pallas kernels  144 us (95%)
  local copies, waits for them, and re-layouts  6.35 us (4%)
    pallas_call x1, Pallas kernels, shards(): pl.pallas_call(kernel, out_shape=(jax.ShapeDtypeStruct(queries.shape, bf)...  144 us
    unnamed x3, local copies, waits for them, and re-layouts  6.35 us

profile of v3, /device:TPU:1, one launch (start us, length us, event | category | flops | bytes accessed | tf_op | source)
XLA Modules:
  0.0 151.1 jit_solution(10986999935434583551)
XLA Ops:
  0.6 1.3 copy.11.no_ref
  2.0 144.1 %cross_attention_back.1 = (bf16[256,1024]{1,0:T(8,128)(2,1)}, bf16[16,64,1024]{2,1,0:T(8,128)(2,1)}) custom-call(s32[64]{0:T(128)} %slots_ref.1, s32[4,2]{1,0:T(4,128)} %copy.11.no_ref, f32[1,128]{1,0:T(1,128)} %bitcast.2, f32[1,128]{1,0:T(1,128)} %bitcast.3, bf16[16,64,1024]{2,1,0:T(8,128)(2,1)} %nb_hbm.1, bf16[1024,1024]{1,0:T(8,128)(2,1)} %wk_hbm.1, ...), custom_call_target="tpu_custom_call" | custom-call | tf_op jit(solution)/shard_map/cross_attention_back/pallas_call | solution.py:464
  146.1 1.9 %copy.14 = bf16[256,1024]{1,0:T(8,128)(2,1)} copy(bf16[256,1024]{1,0:T(8,128)(2,1)} %get-tuple-element.4) | data formatting | bytes 1048576
  148.0 3.1 %copy.15 = bf16[16,64,1024]{2,1,0:T(8,128)(2,1)} copy(bf16[16,64,1024]{2,1,0:T(8,128)(2,1)} %get-tuple-element.5) | data formatting | bytes 4194304

commit v4 on v3

--- a/solution.py
+++ b/solution.py
@@ -135,7 +135,7 @@
     part, yr, gs, r1, fw, rz, fr, placed_ref, meta, mets,
     x_s, x_r, z1_s, z1_r, z2_s, z2_r, y_s, y_r,
     by_s, by_r, r1_s, r1_r, r2_s, r2_r, bx_s, bx_r, out_sem,
-    m_s, m_r, m_l, in_sem, q_sem,
+    e_s, e_r, m_s, m_r, m_l, in_sem, q_sem,
 ):
     x, z, t, g = place()
     chunks = CHUNKS
@@ -154,7 +154,7 @@
     lane8 = lax.broadcasted_iota(jnp.int32, (8, 128), 1)
     row = jnp.zeros((8, 128), jnp.int32)
     for p in range(PER):
-        owner = no_ref[p // 2, p % 2]
+        owner = no_ref[p % 2, p // 2]
         row = jnp.where(lane8 == p, owner, row)
         row = jnp.where(lane8 == PER + owner, p, row)
     meta[1 * NG + g] = row
@@ -182,50 +182,70 @@
     def columns(c):
         return pl.ds(pl.multiple_of(c * wide, wide), wide)
 
-    def stage_x(c):
-        rows = nb[:, :, columns(c)].reshape(size, wide)
-        sent[c] = dot(perm[...], rows, NN).astype(jnp.bfloat16).reshape(NX, NZ, NG, SUB, wide)
-        for dx, _, _, _ in X_PEERS:
-            to = lax.rem(x + dx, NX)
-            push(sent.at[c, to], xr.at[c, :, :, x], x_s.at[c], x_r.at[c], at(to, z, t, g))
-        pltpu.make_async_copy(sent.at[c, x], xr.at[c, :, :, x], x_r.at[c]).start()
-
-    def stage_z1(c):
-        arrive(xr.at[c], x_r.at[c])
+    def stage_x(j):
+        cols = pl.ds(pl.multiple_of(j * 2 * wide, 2 * wide), 2 * wide)
+        sorted_rows = dot(perm[...], nb[:, :, cols].reshape(size, 2 * wide), NN).astype(jnp.bfloat16)
+        for k in range(2):
+            c = 2 * j + k
+            half = sorted_rows[:, k * wide:(k + 1) * wide]
+            sent[c] = half.reshape(NX, NZ, NG, SUB, wide)
+            for dx, _, _, _ in X_PEERS:
+                to = lax.rem(x + dx, NX)
+                push(sent.at[c, to], xr.at[c, NX - dx], x_s.at[c], x_r.at[c], at(to, z, t, g))
+            pltpu.make_async_copy(sent.at[c, x], xr.at[c, 0], x_r.at[c]).start()
+        both = pl.ds(2 * j, 2)
         for way, sign in ((0, 1), (1, -1)):
             for k in (3, 2, 1):
                 dest = lax.rem(z + sign * (k + 1) + NZ, NZ)
                 if k == 3:
-                    src, dst = xr.at[c, dest, way], zb.at[c, way, 4]
+                    src, dst = sent.at[both, x, dest, way], zb.at[both, way, 0, 4]
                 else:
-                    src, dst = xr.at[c, dest], zb.at[c, way, pl.ds(2 * (k - 1), 2)]
+                    src, dst = sent.at[both, x, dest], zb.at[both, way, 0, pl.ds(2 * (k - 1), 2)]
+                push(src, dst, e_s.at[j], e_r.at[j], at(x, z + sign * k, t, g))
+
+    def stage_z1(c):
+        arrive(xr.at[c], x_r.at[c])
+        others = pl.ds(1, NX - 1)
+        for way, sign in ((0, 1), (1, -1)):
+            for k in (3, 2, 1):
+                dest = lax.rem(z + sign * (k + 1) + NZ, NZ)
+                if k == 3:
+                    src, dst = xr.at[c, others, dest, way], zb.at[c, way, others, 4]
+                else:
+                    src, dst = xr.at[c, others, dest], zb.at[c, way, others, pl.ds(2 * (k - 1), 2)]
                 push(src, dst, z1_s.at[c], z1_r.at[c], at(x, z + sign * k, t, g))
 
+    def column(owner):
+        return lax.rem(owner // NZ - x + NX, NX)
+
     def stage_z2(c):
-        arrive(zb.at[c], z1_r.at[c])
+        @pl.when(lax.rem(c, 2) == 0)
+        def _():
+            arrive(zb.at[pl.ds(c, 2), :, 0], e_r.at[c // 2])
+        arrive(zb.at[c, :, pl.ds(1, NX - 1)], z1_r.at[c])
         for way, sign in ((0, 1), (1, -1)):
             dest = lax.rem(z + sign + NZ, NZ)
             for h in range(NG):
                 far = 3 if h == way else 2
-                tiles = [xr[c, dest, h, xo] for xo in range(NX)]
+                tiles = [xr[c, k, dest, h] for k in range(NX)]
                 for k in range(1, far + 1):
                     part = 4 if k == 3 else 2 * (k - 1) + h
-                    tiles += [zb[c, way, part, xo] for xo in range(NX)]
+                    tiles += [zb[c, way, j, part] for j in range(NX)]
                 for p in range(PER):
                     owner = mets[(1 + sign) * NG + h, 0, p]
                     rel = lax.rem(sign * (z - lax.rem(owner, NZ)) + NZ, NZ)
-                    mg[c, way, h, p] = choose(tiles, range(len(tiles)), rel * NX + owner // NZ)
+                    mg[c, way, h, p] = choose(tiles, range(len(tiles)), rel * NX + column(owner))
             push(mg.at[c, way], zr.at[c, way], z2_s.at[c], z2_r.at[c], at(x, z + sign, t, g))
 
     def stage_y(c):
         arrive(mg.at[c], z2_r.at[c])
         for h in range(NG):
-            own = [xr[c, z, h, xo] for xo in range(NX)]
+            own = [xr[c, k, z, h] for k in range(NX)]
             for p in range(PER):
                 owner = mets[NG + h, 0, p]
                 rel = lax.rem(z - lax.rem(owner, NZ) + NZ, NZ)
                 back = jnp.where(rel >= (5 if h == 0 else 4), zr[c, 1, h, p], zr[c, 0, h, p])
-                near = choose(own, range(NX), owner // NZ)
+                near = choose(own, range(NX), column(owner))
                 fin[c, h, p] = jnp.where(rel == 0, near, back)
         slot = t * NG + g
         for _, _, dt, dg in Y_PEERS:
@@ -264,35 +284,20 @@
         def _():
             project(c // 2)
 
+    for j in range(chunks // 2):
+        stage_x(j)
+    arrive(meta.at[pl.ds(0, 5)], m_r)
+    copy = pltpu.make_async_copy(meta, mets, m_l)
+    copy.start()
+    copy.wait()
+
     def step(i, carry):
-        @pl.when(i < chunks)
-        def _():
-            stage_x(i)
-
-        @pl.when((i >= 1) & (i <= chunks))
-        def _():
-            stage_z1(i - 1)
-
-        @pl.when(i == 1)
-        def _():
-            arrive(meta.at[pl.ds(0, 5)], m_r)
-            copy = pltpu.make_async_copy(meta, mets, m_l)
-            copy.start()
-            copy.wait()
-
-        @pl.when((i >= 2) & (i <= chunks + 1))
-        def _():
-            stage_z2(i - 2)
-
-        @pl.when((i >= 3) & (i <= chunks + 2))
-        def _():
-            stage_y(i - 3)
-
-        @pl.when(i >= 4)
-        def _():
-            stage_p(i - 4)
+        for lag, stage in ((0, stage_z1), (2, stage_z2), (3, stage_y), (5, stage_p)):
+            @pl.when((i >= lag) & (i < chunks + lag))
+            def _(stage=stage, lag=lag):
+                stage(i - lag)
         return carry
-    lax.fori_loop(0, chunks + 4, step, 0)
+    lax.fori_loop(0, chunks + 5, step, 0)
 
     attend(enc, kacc, vacc, wk, wv, q, go, qg_ref, kg_ref, qgrad, dkr, dv)
     give = pltpu.make_async_copy(qgrad, qgrad_hbm, q_sem)
@@ -366,10 +371,10 @@
         pltpu.make_async_copy(placed_ref.at[c], out_hbm.at[:, :, columns(c)], out_sem.at[c]).start()
 
     def back_step(i, carry):
-        for k, stage in enumerate((back_y, back_r1, back_r2, back_x, back_out)):
-            @pl.when((i >= k) & (i < chunks + k))
-            def _(stage=stage, k=k):
-                stage(i - k)
+        for lag, stage in ((4, back_r2), (2, back_r1), (0, back_y), (5, back_x), (6, back_out)):
+            @pl.when((i >= lag) & (i < chunks + lag))
+            def _(stage=stage, lag=lag):
+                stage(i - lag)
 
         @pl.when(i == 0)
         def _():
@@ -386,11 +391,11 @@
             for k in range(size // 128):
                 perm_back[:, k * 128:(k + 1) * 128] = (order + k * 128 == rows).astype(jnp.bfloat16)
         return carry
-    lax.fori_loop(0, chunks + 4, back_step, 0)
+    lax.fori_loop(0, chunks + 6, back_step, 0)
 
     def drain(c, carry):
         arrive(sent.at[c, pl.ds(0, 3)], x_s.at[c])
-        arrive(zb.at[c], z1_s.at[c])
+        arrive(zb.at[c, :, pl.ds(1, NX - 1)], z1_s.at[c])
         arrive(mg.at[c], z2_s.at[c])
         arrive(part.at[c, pl.ds(0, 7)], y_s.at[c])
         arrive(part.at[c, pl.ds(0, 7)], by_s.at[c])
@@ -400,8 +405,29 @@
         pltpu.make_async_copy(placed_ref.at[c], out_hbm.at[:, :, columns(c)], out_sem.at[c]).wait()
         return carry
     lax.fori_loop(0, chunks, drain, 0)
+    for j in range(chunks // 2):
+        arrive(zb.at[pl.ds(2 * j, 2), :, 0], e_s.at[j])
     arrive(meta.at[pl.ds(0, 5)], m_s)
     give.wait()
+
+
+def settle_kernel(a_ref, b_ref, x_ref, y_ref):
+    x_ref[...] = a_ref[...]
+    y_ref[...] = b_ref[...]
+
+
+def settle(a, b):
+    steps = 4
+    a_spec = pl.BlockSpec((a.shape[0] // steps, a.shape[1]), lambda i: (i, 0))
+    b_spec = pl.BlockSpec((b.shape[0] // steps,) + b.shape[1:], lambda i: (i, 0, 0))
+    return pl.pallas_call(
+        settle_kernel,
+        grid=(steps,),
+        out_shape=(jax.ShapeDtypeStruct(a.shape, a.dtype), jax.ShapeDtypeStruct(b.shape, b.dtype)),
+        in_specs=[a_spec, b_spec],
+        out_specs=(a_spec, b_spec),
+        name="settle",
+    )(a, b)
 
 
 def shards(
@@ -439,8 +465,8 @@
         pltpu.VMEM((size, size), bf),
         pltpu.VMEM((size, size), bf),
         tiles(NX, NZ, NG),
-        tiles(NZ, NG, NX),
-        tiles(2, 5, NX),
+        tiles(NX, NZ, NG),
+        tiles(2, NX, 5),
         tiles(2, NG, PER),
         tiles(2, NG, PER),
         tiles(NG, PER),
@@ -460,8 +486,8 @@
         pltpu.VMEM((3 * NG, 8, 128), jnp.int32),
         pltpu.SMEM((3 * NG, 8, 128), jnp.int32),
     ]
-    scratch += [dma((CHUNKS,))] * 17 + [dma, dma, dma, dma((5,)), dma]
-    return pl.pallas_call(
+    scratch += [dma((CHUNKS,))] * 17 + [dma((CHUNKS // 2,))] * 2 + [dma, dma, dma, dma((5,)), dma]
+    query_grad, neighbour_grad = pl.pallas_call(
         kernel,
         out_shape=(
             jax.ShapeDtypeStruct(queries.shape, bf),
@@ -475,9 +501,10 @@
             collective_id=0, has_side_effects=True, vmem_limit_bytes=60 * 2**20
         ),
     )(
-        owner_slots, neighbour_owner, query_gain.reshape(1, HD), key_gain.reshape(1, HD),
+        owner_slots, neighbour_owner.T, query_gain.reshape(1, HD), key_gain.reshape(1, HD),
         neighbours, key_weight, value_weight, queries, out_grad,
     )
+    return settle(query_grad, neighbour_grad)
 
 
 def solution(mesh):

time: 151 us -> 140 us (0.927)
  local copies, waits for them, and re-layouts: 6.35 us -> 0 us
  Pallas kernels: 144 us -> 139 us
    pallas_call x1, Pallas kernels: 144 us -> 135 us  [shards(): pl.pallas_call(kernel, out_shape=(jax.ShapeDtypeStruct(queries.shape, bf)...]
    unnamed x3 -> x0, local copies, waits for them, and re-layouts: 6.35 us -> none
    pallas_call x0 -> x1, Pallas kernels: none -> 4.01 us  [settle(): pl.pallas_call(settle_kernel, grid=(steps,), out_shape=(jax.ShapeDtypeStr...]
where the time goes in v4:
time: 140 us
  Pallas kernels  139 us (99%)
    pallas_call x1, Pallas kernels, shards(): pl.pallas_call(kernel, out_shape=(jax.ShapeDtypeStruct(queries.shape, bf)...  135 us
    pallas_call x1, Pallas kernels, settle(): pl.pallas_call(settle_kernel, grid=(steps,), out_shape=(jax.ShapeDtypeStr...  4.01 us

profile of v4, /device:TPU:1, one launch (start us, length us, event | category | flops | bytes accessed | tf_op | source)
XLA Modules:
  0.0 140.1 jit_solution(5549063861285457334)
XLA Ops:
  0.6 135.4 %cross_attention_back.1 = (bf16[256,1024]{1,0:T(8,128)(2,1)}, bf16[16,64,1024]{2,1,0:T(8,128)(2,1)}) custom-call(s32[64]{0:T(128)} %slots_ref.1, s32[2,4]{1,0:T(2,128)} %bitcast.3, f32[1,128]{1,0:T(1,128)} %bitcast.4, f32[1,128]{1,0:T(1,128)} %bitcast.5, bf16[16,64,1024]{2,1,0:T(8,128)(2,1)} %nb_hbm.1, bf16[1024,1024]{1,0:T(8,128)(2,1)} %wk_hbm.1, ...), custom_call_target="tpu_custom_call" | custom-call | tf_op jit(solution)/shard_map/cross_attention_back/pallas_call | solution.py:490
  136.1 4.0 %settle.1 = (bf16[256,1024]{1,0:T(8,128)(2,1)}, bf16[16,64,1024]{2,1,0:T(8,128)(2,1)}) custom-call(bf16[256,1024]{1,0:T(8,128)(2,1)} %get-tuple-element.4.a_ref, bf16[16,64,1024]{2,1,0:T(8,128)(2,1)} %get-tuple-element.5.b_ref), custom_call_target="tpu_custom_call" | custom-call | tf_op jit(solution)/shard_map/settle/pallas_call | solution.py:423

commit v5 on v4

--- a/solution.py
+++ b/solution.py
@@ -69,7 +69,7 @@
     return result
 
 
-def attend(e_ref, kacc, vacc, wk_ref, wv_ref, q_ref, go_ref, qg_ref, kg_ref, qgrad_ref, dkr_ref, dv_ref):
+def attend(done, e_ref, kacc, vacc, wk_ref, wv_ref, q_ref, go_ref, qg_ref, kg_ref, qgrad_ref, dkr_ref, dv_ref):
     rows, width = q_ref.shape
     stretches = rows // CH
     groups, per_dev, sub, enc = e_ref.shape
@@ -79,8 +79,8 @@
 
     def pair(i, carry):
         cols = pl.ds(pl.multiple_of(i * 2 * HD, 2 * HD), 2 * HD)
-        last = slice(enc - 256, enc)
-        enc_rows = e_ref[:, :, :, last].reshape(groups * per_dev * sub, 256)
+        last = slice(done, enc)
+        enc_rows = e_ref[:, :, :, last].reshape(groups * per_dev * sub, enc - done)
         kr2 = kacc[:, cols] + dot(enc_rows, wk_ref[last, cols], NN)
         val2 = (vacc[:, cols] + dot(enc_rows, wv_ref[last, cols], NN)).astype(jnp.bfloat16)
         for hh in range(2):
@@ -98,33 +98,43 @@
             qhat = qx * qinv
             qn = (qhat * qgain).astype(jnp.bfloat16)
             go = go_ref[:, head]
-            for c in range(stretches):
-                tok = slice(c * CH, (c + 1) * CH)
-                kn_c = kn[:, 2 * c:2 * c + 2].reshape(keys, HD)
-                val_c = val[:, 2 * c:2 * c + 2].reshape(keys, HD)
-                qn_c, go_c = qn[tok], go[tok]
-                weights = jnp.exp(dot(qn_c, kn_c, NT) * SCALE)
+            kn_s = [kn[:, 2 * c:2 * c + 2].reshape(keys, HD) for c in range(stretches)]
+            val_s = [val[:, 2 * c:2 * c + 2].reshape(keys, HD) for c in range(stretches)]
+            toks = [slice(c * CH, (c + 1) * CH) for c in range(stretches)]
+            scores = [dot(qn[toks[c]], kn_s[c], NT) for c in range(stretches)]
+            dps = [dot(go[toks[c]], val_s[c], NT) for c in range(stretches)]
+            half = lax.broadcasted_iota(jnp.int32, (2 * CH, HD), 0) < CH
+            zero = jnp.zeros((2 * CH, HD), jnp.bfloat16)
+            for j in range(stretches // 2):
+                two = slice(j * 2 * CH, (j + 1) * 2 * CH)
+                score = jnp.concatenate(scores[2 * j:2 * j + 2], axis=0)
+                dp = jnp.concatenate(dps[2 * j:2 * j + 2], axis=0)
+                weights = jnp.exp(score * SCALE)
                 prob = weights * (1.0 / jnp.sum(weights, axis=-1, keepdims=True))
-                dp = dot(go_c, val_c, NT)
                 inner = jnp.sum(prob * dp, axis=-1, keepdims=True)
                 ds = (prob * (dp - inner)).astype(jnp.bfloat16)
                 pb = prob.astype(jnp.bfloat16)
-                dv_c = dot(pb, go_c, TN).astype(jnp.bfloat16)
-                dkn = dot(ds, qn_c, TN)
-                dqn = dot(ds, kn_c, NN)
+                go_2, qn_2 = go[two], qn[two]
+                go_b = jnp.concatenate([jnp.where(half, go_2, zero), jnp.where(half, zero, go_2)], axis=1)
+                qn_b = jnp.concatenate([jnp.where(half, qn_2, zero), jnp.where(half, zero, qn_2)], axis=1)
+                dv2 = dot(pb, go_b, TN).astype(jnp.bfloat16)
+                dkn2 = dot(ds, qn_b, TN)
+                dqn = jnp.concatenate([dot(ds[k * CH:(k + 1) * CH], kn_s[2 * j + k], NN) for k in range(2)], axis=0)
                 qs = dqn * (qgain * SCALE)
-                qh = qhat[tok]
+                qh = qhat[two]
                 qi = jnp.mean(qh * qs, axis=-1, keepdims=True)
-                qgrad_ref[tok, head] = (qinv[tok] * (qs - qh * qi)).astype(jnp.bfloat16)
-                ks = dkn * (kgain * SCALE)
-                kh = khat[:, 2 * c:2 * c + 2].reshape(keys, HD)
-                ki = jnp.mean(kh * ks, axis=-1, keepdims=True)
-                kv = kinv[:, 2 * c:2 * c + 2].reshape(keys, 1)
-                dk = (kv * (ks - kh * ki)).astype(jnp.bfloat16)
-                dkr_ref[:, 2 * c:2 * c + 2, :, head] = dk.reshape(groups, 2, sub, HD)
-                dv_ref[:, 2 * c:2 * c + 2, :, head] = dv_c.reshape(groups, 2, sub, HD)
+                qgrad_ref[two, head] = (qinv[two] * (qs - qh * qi)).astype(jnp.bfloat16)
+                for k in range(2):
+                    part = slice(2 * (2 * j + k), 2 * (2 * j + k) + 2)
+                    ks = dkn2[:, k * HD:(k + 1) * HD] * (kgain * SCALE)
+                    kh = khat[:, part].reshape(keys, HD)
+                    ki = jnp.mean(kh * ks, axis=-1, keepdims=True)
+                    kv = kinv[:, part].reshape(keys, 1)
+                    dk = (kv * (ks - kh * ki)).astype(jnp.bfloat16)
+                    dkr_ref[:, part, :, head] = dk.reshape(groups, 2, sub, HD)
+                    dv_ref[:, part, :, head] = dv2[:, k * HD:(k + 1) * HD].reshape(groups, 2, sub, HD)
         return carry
-    lax.fori_loop(0, width // (2 * HD), pair, 0)
+    lax.fori_loop(0, width // (2 * HD), pair, 0, unroll=2)
 
 
 def kernel(
@@ -180,6 +190,8 @@
     loads[0].wait()
 
     def columns(c):
+        if isinstance(c, int):
+            return pl.ds(c * wide, wide)
         return pl.ds(pl.multiple_of(c * wide, wide), wide)
 
     def stage_x(j):
@@ -193,6 +205,8 @@
                 to = lax.rem(x + dx, NX)
                 push(sent.at[c, to], xr.at[c, NX - dx], x_s.at[c], x_r.at[c], at(to, z, t, g))
             pltpu.make_async_copy(sent.at[c, x], xr.at[c, 0], x_r.at[c]).start()
+
+    def stage_e(j):
         both = pl.ds(2 * j, 2)
         for way, sign in ((0, 1), (1, -1)):
             for k in (3, 2, 1):
@@ -253,53 +267,40 @@
             push(fin.at[c, to], enc.at[slot, :, :, columns(c)], y_s.at[c], y_r.at[c], at(x, z, t + dt, to))
         pltpu.make_async_copy(fin.at[c, g], enc.at[slot, :, :, columns(c)], y_r.at[c]).start()
 
-    def project(j):
-        rows = pl.ds(pl.multiple_of(j * 256, 256), 256)
-        left = enc[:, :, :, rows].reshape(size, 256)
-
+    def project(deep):
         def block_of(k, carry):
             cols = pl.ds(pl.multiple_of(k * 256, 256), 256)
-            for acc, weight in ((kacc, wk), (vacc, wv)):
-                term = dot(left, weight[rows, cols], NN)
-
-                @pl.when(j == 0)
-                def _(acc=acc, term=term):
-                    acc[:, cols] = term
-
-                @pl.when(j > 0)
-                def _(acc=acc, term=term):
-                    acc[:, cols] += term
+            left = enc[:, :, :, :deep].reshape(size, deep)
+            kacc[:, cols] = dot(left, wk[:deep, cols], NN)
+            vacc[:, cols] = dot(left, wv[:deep, cols], NN)
             return carry
         lax.fori_loop(0, wk.shape[1] // 256, block_of, 0)
 
-    def stage_p(c):
-        arrive(enc.at[:, :, :, columns(c)], y_r.at[c])
-
-        @pl.when(c == 0)
-        def _():
-            for load in loads[1:]:
-                load.wait()
-
-        @pl.when((lax.rem(c, 2) == 1) & (c < chunks - 1))
-        def _():
-            project(c // 2)
-
     for j in range(chunks // 2):
         stage_x(j)
+        stage_e(j)
     arrive(meta.at[pl.ds(0, 5)], m_r)
     copy = pltpu.make_async_copy(meta, mets, m_l)
     copy.start()
     copy.wait()
 
     def step(i, carry):
-        for lag, stage in ((0, stage_z1), (2, stage_z2), (3, stage_y), (5, stage_p)):
+        for lag, stage in ((0, stage_z1), (1, stage_z2), (2, stage_y)):
             @pl.when((i >= lag) & (i < chunks + lag))
             def _(stage=stage, lag=lag):
                 stage(i - lag)
         return carry
-    lax.fori_loop(0, chunks + 5, step, 0)
-
-    attend(enc, kacc, vacc, wk, wv, q, go, qg_ref, kg_ref, qgrad, dkr, dv)
+    lax.fori_loop(0, chunks + 2, step, 0)
+    for load in loads[1:]:
+        load.wait()
+    early = 6
+    for c in range(early):
+        arrive(enc.at[:, :, :, columns(c)], y_r.at[c])
+    project(early * wide)
+    for c in range(early, chunks):
+        arrive(enc.at[:, :, :, columns(c)], y_r.at[c])
+
+    attend(early * wide, enc, kacc, vacc, wk, wv, q, go, qg_ref, kg_ref, qgrad, dkr, dv)
     give = pltpu.make_async_copy(qgrad, qgrad_hbm, q_sem)
     give.start()
 
@@ -417,7 +418,7 @@
 
 
 def settle(a, b):
-    steps = 4
+    steps = 2
     a_spec = pl.BlockSpec((a.shape[0] // steps, a.shape[1]), lambda i: (i, 0))
     b_spec = pl.BlockSpec((b.shape[0] // steps,) + b.shape[1:], lambda i: (i, 0, 0))
     return pl.pallas_call(

time: 140 us -> 125 us (0.89)
  Pallas kernels: 139 us -> 124 us
    pallas_call x1, Pallas kernels: 135 us -> 121 us  [shards(): pl.pallas_call(kernel, out_shape=(jax.ShapeDtypeStruct(queries.shape, bf)...]
where the time goes in v5:
time: 125 us
  Pallas kernels  124 us (99%)
    pallas_call x1, Pallas kernels, shards(): pl.pallas_call(kernel, out_shape=(jax.ShapeDtypeStruct(queries.shape, bf)...  121 us
    pallas_call x1, Pallas kernels, settle(): pl.pallas_call(settle_kernel, grid=(steps,), out_shape=(jax.ShapeDtypeStr...  2.9 us

profile of v5, /device:TPU:1, one launch (start us, length us, event | category | flops | bytes accessed | tf_op | source)
XLA Modules:
  0.0 124.6 jit_solution(16160294319344603956)
XLA Ops:
  0.6 121.0 %cross_attention_back.1 = (bf16[256,1024]{1,0:T(8,128)(2,1)}, bf16[16,64,1024]{2,1,0:T(8,128)(2,1)}) custom-call(s32[64]{0:T(128)} %slots_ref.1, s32[2,4]{1,0:T(2,128)} %bitcast.3, f32[1,128]{1,0:T(1,128)} %bitcast.4, f32[1,128]{1,0:T(1,128)} %bitcast.5, bf16[16,64,1024]{2,1,0:T(8,128)(2,1)} %nb_hbm.1, bf16[1024,1024]{1,0:T(8,128)(2,1)} %wk_hbm.1, ...), custom_call_target="tpu_custom_call" | custom-call | tf_op jit(solution)/shard_map/cross_attention_back/pallas_call | solution.py:491
  121.7 2.9 %settle.1 = (bf16[256,1024]{1,0:T(8,128)(2,1)}, bf16[16,64,1024]{2,1,0:T(8,128)(2,1)}) custom-call(bf16[256,1024]{1,0:T(8,128)(2,1)} %get-tuple-element.4.a_ref, bf16[16,64,1024]{2,1,0:T(8,128)(2,1)} %get-tuple-element.5.b_ref), custom_call_target="tpu_custom_call" | custom-call | tf_op jit(solution)/shard_map/settle/pallas_call | solution.py:424

commit v6 on v5

--- a/solution.py
+++ b/solution.py
@@ -279,6 +279,18 @@
     for j in range(chunks // 2):
         stage_x(j)
         stage_e(j)
+    across = lax.broadcasted_iota(jnp.int32, (size, 128), 1)
+    down = lax.broadcasted_iota(jnp.int32, (8, 128), 0)
+    parts = []
+    for k in range(slots // 8):
+        value = jnp.zeros((8, 128), jnp.int32)
+        for s in range(8):
+            value = jnp.where(down == s, block(k * 8 + s), value)
+        parts.append(value)
+    rows = jnp.concatenate(parts, axis=0)
+    rows = jnp.concatenate([rows + r for r in range(SUB)], axis=0)
+    for k in range(size // 128):
+        perm_back[:, k * 128:(k + 1) * 128] = (across + k * 128 == rows).astype(jnp.bfloat16)
     arrive(meta.at[pl.ds(0, 5)], m_r)
     copy = pltpu.make_async_copy(meta, mets, m_l)
     copy.start()
@@ -377,20 +389,6 @@
             def _(stage=stage, lag=lag):
                 stage(i - lag)
 
-        @pl.when(i == 0)
-        def _():
-            order = lax.broadcasted_iota(jnp.int32, (size, 128), 1)
-            down = lax.broadcasted_iota(jnp.int32, (8, 128), 0)
-            parts = []
-            for k in range(slots // 8):
-                value = jnp.zeros((8, 128), jnp.int32)
-                for s in range(8):
-                    value = jnp.where(down == s, block(k * 8 + s), value)
-                parts.append(value)
-            rows = jnp.concatenate(parts, axis=0)
-            rows = jnp.concatenate([rows + r for r in range(SUB)], axis=0)
-            for k in range(size // 128):
-                perm_back[:, k * 128:(k + 1) * 128] = (order + k * 128 == rows).astype(jnp.bfloat16)
         return carry
     lax.fori_loop(0, chunks + 6, back_step, 0)
 
@@ -412,22 +410,41 @@
     give.wait()
 
 
-def settle_kernel(a_ref, b_ref, x_ref, y_ref):
-    x_ref[...] = a_ref[...]
-    y_ref[...] = b_ref[...]
+def settle_kernel(a_ref, b_ref, x_ref, y_ref, a_held, b_held, in_sem, out_sem):
+    moves = []
+    for src, held, dst, pieces in ((b_ref, b_held, y_ref, 8), (a_ref, a_held, x_ref, 2)):
+        rows = src.shape[0] // pieces
+        for k in range(pieces):
+            part = pl.ds(k * rows, rows)
+            n = len(moves)
+            moves.append((
+                pltpu.make_async_copy(src.at[part], held.at[part], in_sem.at[n]),
+                pltpu.make_async_copy(held.at[part], dst.at[part], out_sem.at[n]),
+            ))
+    for load, _ in moves:
+        load.start()
+    for load, store in moves:
+        load.wait()
+        store.start()
+    for _, store in moves:
+        store.wait()
 
 
 def settle(a, b):
-    steps = 2
-    a_spec = pl.BlockSpec((a.shape[0] // steps, a.shape[1]), lambda i: (i, 0))
-    b_spec = pl.BlockSpec((b.shape[0] // steps,) + b.shape[1:], lambda i: (i, 0, 0))
+    hbm = pl.BlockSpec(memory_space=pl.ANY)
     return pl.pallas_call(
         settle_kernel,
-        grid=(steps,),
         out_shape=(jax.ShapeDtypeStruct(a.shape, a.dtype), jax.ShapeDtypeStruct(b.shape, b.dtype)),
-        in_specs=[a_spec, b_spec],
-        out_specs=(a_spec, b_spec),
+        in_specs=[hbm, hbm],
+        out_specs=(hbm, hbm),
+        scratch_shapes=[
+            pltpu.VMEM(a.shape, a.dtype),
+            pltpu.VMEM(b.shape, b.dtype),
+            pltpu.SemaphoreType.DMA((10,)),
+            pltpu.SemaphoreType.DMA((10,)),
+        ],
         name="settle",
+        compiler_params=pltpu.CompilerParams(vmem_limit_bytes=60 * 2**20),
     )(a, b)
 
 

time: 125 us -> 124 us (level)
  no operation moved by 1% of the time
where the time goes in v6:
time: 124 us
  Pallas kernels  124 us (100%)
    pallas_call x1, Pallas kernels, shards(): pl.pallas_call(kernel, out_shape=(jax.ShapeDtypeStruct(queries.shape, bf)...  121 us
    pallas_call x1, Pallas kernels, settle(): pl.pallas_call(settle_kernel, out_shape=(jax.ShapeDtypeStruct(a.shape, a....  2.6 us

profile of v6, /device:TPU:1, one launch (start us, length us, event | category | flops | bytes accessed | tf_op | source)
XLA Modules:
  0.0 124.3 jit_solution(9149114705906717115)
XLA Ops:
  0.6 121.0 %cross_attention_back.1 = (bf16[256,1024]{1,0:T(8,128)(2,1)}, bf16[16,64,1024]{2,1,0:T(8,128)(2,1)}) custom-call(s32[64]{0:T(128)} %slots_ref.1, s32[2,4]{1,0:T(2,128)} %bitcast.3, f32[1,128]{1,0:T(1,128)} %bitcast.4, f32[1,128]{1,0:T(1,128)} %bitcast.5, bf16[16,64,1024]{2,1,0:T(8,128)(2,1)} %nb_hbm.1, bf16[1024,1024]{1,0:T(8,128)(2,1)} %wk_hbm.1, ...), custom_call_target="tpu_custom_call" | custom-call | tf_op jit(solution)/shard_map/cross_attention_back/pallas_call | solution.py:508
  121.7 2.6 %settle.1 = (bf16[256,1024]{1,0:T(8,128)(2,1)}, bf16[16,64,1024]{2,1,0:T(8,128)(2,1)}) custom-call(bf16[256,1024]{1,0:T(8,128)(2,1)} %get-tuple-element.4.a_ref, bf16[16,64,1024]{2,1,0:T(8,128)(2,1)} %get-tuple-element.5.b_ref), custom_call_target="tpu_custom_call" | custom-call | tf_op jit(solution)/shard_map/settle/pallas_call | solution.py:435
